TPU v7x, 256 devices: a whole 4x4x8 slice. The times are simulated.
256 devices in a mesh: gx: 8 (over x, z_lo), gy: 4 (over y), gz: 8 (over z_hi, core).
Axes of the slice: x: 4, y: 4, z: 8 (z_hi: 4, z_lo: 2; z = z_hi * 2 + z_lo), core: 2. Of those that a mesh axis runs over, the one named last changes fastest.
Arguments:
- states: float32 [19, 128, 64, 1024], P(None, 'gx', 'gy', 'gz'), may hold values from 0 to 1
- active: int32 [16, 4, 8], P('gx', 'gy', 'gz'), may hold values 0 or 1
- fibre_index: int32 [16, 4, 8], P('gx', 'gy', 'gz'), may hold values from 0 to 63
- fibre_angle: float32 [2, 64], replicated, may hold values from -3.140625 to 3.140625
- conduct: float32 [2, 64], replicated, may hold values from 0.05 to 0.3
- gate_half: float32 [17], replicated, may hold values from 0.1 to 0.9
- gate_slope: float32 [17], replicated, may hold values from 0.05 to 0.3
- gate_tau: float32 [17], replicated, may hold values from 2 to 60
- conductance: float32 [17], replicated, may hold values from 0.005 to 0.05
- reversal: float32 [17], replicated, may hold values from -1 to 1.5
- block_elem: int32 [64, 32, 32], P('gx', 'gy', 'gz'), may hold values from 0 to 65535, as said below
- block_weight: float32 [64, 32, 32], P('gx', 'gy', 'gz'), may hold values from 0.5 to 1.5
- node_disp: float32 [3, 131072], P(None, ('gx', 'gy', 'gz')), may hold values from -0.15 to 0.15
- elem_node: int32 [8, 65536], P(None, ('gx', 'gy', 'gz')), may hold values from 0 to 404, as said below
- elem_fibre: int32 [65536], P(('gx', 'gy', 'gz')), may hold values from 0 to 63
- material: float32 [3], replicated, may hold values from 0.5 to 2
Outputs:
- new_states: float32 [19, 128, 64, 1024], P(None, 'gx', 'gy', 'gz')
- fine_disp: float32 [3, 128, 64, 1024], P(None, 'gx', 'gy', 'gz')
- node_residual: float32 [3, 131072], P(None, ('gx', 'gy', 'gz'))
Inputs may be any that keep to these rules, and one draw needn't show every extreme that they name: `block_elem`: element numbers of the coarse partition: owner device e // 256, local element e % 256. Every element holds exactly one coupling block. Of the coupling blocks of one device at most 2 lie in elements of one owner device, and for every device some owner receives exactly 2 of them. `elem_node`: each column names eight distinct owner-local nodes of a hexahedral element of a structured partition, corner 4 i + 2 j + k at offset (i, j, k); neighbouring elements of one owner share nodes.
All inputs are finite; a program needn't handle non-finite values. No bound on the sum of `active` on one device may be relied on, other than what follows from the above.
Results may differ from a plain program's by a relative error of at most 0.0003.
Values sent between devices are 32-bit elements; how exact they have to be, the bound alone decides.
No kernel may reach another device: no remote copies, remote signals or barrier semaphores. Data moves between devices by JAX's collectives and lax.ppermute only.
A program may use at most 64 MiB of HBM per device.

v0:
```python
import functools

import jax
import jax.numpy as jnp
import numpy as np
from jax import lax
from jax.experimental import pallas as pl
from jax.experimental.pallas import tpu as pltpu
from jax.sharding import PartitionSpec as P

NSTATE, NCH, NF = 19, 17, 64
CX, CY, CZ = 16, 16, 128
ELEMS, SLOTS, NODES = 256, 256, 512
ALL = ("gx", "gy", "gz")
HIGHEST = lax.Precision.HIGHEST
F32, BF16 = jnp.float32, jnp.bfloat16
NT = (((1,), (1,)), ((), ()))
TN = (((0,), (0,)), ((), ()))
CORNERS = [(q // 4, q // 2 % 2, q % 2) for q in range(8)]
HEAD = 2


def iota(shape, dim):
    return lax.broadcasted_iota(jnp.int32, shape, dim)


def neighbour(pos_ref, sizes, step):
    at = [pos_ref[d] + step[d] for d in range(3)]
    ok = (at[0] >= 0) & (at[0] < sizes[0])
    for d in (1, 2):
        ok = ok & (at[d] >= 0) & (at[d] < sizes[d])
    row = (at[0] * sizes[1] + at[1]) * sizes[2] + at[2]
    return jnp.where(ok, row, 0), ok


def put_row(msg, row, ok, edge):
    base = pl.ds(pl.multiple_of(row // 8 * 8, 8), 8)
    here = iota((8, 128), 0) == jnp.where(ok, row % 8, -1)
    msg[base, 128:256] = jnp.where(here, edge, msg[base, 128:256])


def take_row(got, row, ok, lanes):
    rows = got[pl.ds(pl.multiple_of(row // 8 * 8, 8), 8), lanes]
    here = iota((8, 128), 0) == jnp.where(ok, row % 8, -1)
    return jnp.sum(jnp.where(here, rows, 0.0), axis=0, keepdims=True)


def parts3(x):
    first = x.astype(BF16)
    rest = x - first.astype(F32)
    second = rest.astype(BF16)
    third = (rest - second.astype(F32)).astype(BF16)
    return first, second, third


def frame_of(angles):
    a, b = angles[0:1, :], angles[1:2, :]
    return jnp.cos(a) * jnp.cos(b), jnp.sin(a) * jnp.cos(b), jnp.sin(b)


def gate_constants(half_ref, slope_ref, tau_ref, cond_ref, rev_ref, const):
    for c in range(NCH):
        scale = 0.5 / jnp.full((8, 128), slope_ref[c], F32)
        keep = jnp.exp(-1.0 / jnp.full((8, 128), tau_ref[c], F32))
        cond = jnp.full((8, 128), cond_ref[c], F32)
        const[c] = scale
        const[NCH + c] = -half_ref[c] * scale
        const[2 * NCH + c] = keep
        const[3 * NCH + c] = 0.5 * (1.0 - keep)
        const[4 * NCH + c] = cond
        const[5 * NCH + c] = cond * rev_ref[c]


def twice(x):
    return jnp.concatenate([x, x], 0)


def ionic_plane(volt, source, target, x, alive, const):
    total = jnp.zeros_like(volt)
    moment = jnp.zeros_like(volt)
    for c in range(NCH):
        rise = jnp.tanh(volt * twice(const[c]) + twice(const[NCH + c]))
        old = source[1 + c, x]
        lift = twice(const[3 * NCH + c])
        gate = old * twice(const[2 * NCH + c]) + (lift * rise + lift)
        total += gate * twice(const[4 * NCH + c])
        moment += gate * twice(const[5 * NCH + c])
        target[1 + c, x] = jnp.where(alive, gate, old)
    vstar = volt - (volt * total - moment)
    old = source[NSTATE - 1, x]
    calcium = old * 0.9 + 0.1 * (0.5 * jnp.tanh(4.0 * (volt - 0.5)) + 0.5)
    calcium = jnp.where(alive, calcium, old)
    target[NSTATE - 1, x] = calcium
    return jnp.where(alive, vstar, volt), calcium


def send_faces(v, pos_ref, sizes, xlo, xhi, ylo, yhi, zlo, zhi, msg, lines):
    xlo[...] = v[0:2]
    xhi[...] = v[14:16]
    ylo[...] = v[:, 0:8, :]
    yhi[...] = v[:, 8:16, :]
    row, lane = iota((8, 128), 0), iota((8, 128), 1)
    pick = ((row < 4) & (lane == jnp.where(row < 2, row, row + 124))).astype(F32)
    flat = v[...].reshape(CX * CY, CZ)
    ends = lax.dot_general(pick, flat, NT, precision=HIGHEST, preferred_element_type=F32)
    zlo[...] = ends[0:2]
    zhi[...] = ends[2:4]
    lines[0:16] = v[0]
    lines[16:32] = v[15]
    for x in range(CX):
        lines[32 + x : 33 + x] = v[x, 0:1, :]
        lines[48 + x : 49 + x] = v[x, 15:16, :]
    lines[64:128] = jnp.zeros((64, 128), F32)
    marks = lax.dot_general(pick, lines[...], NT, precision=HIGHEST, preferred_element_type=F32)
    for dx in (-1, 1):
        for dy in (-1, 1):
            peer, ok = neighbour(pos_ref, sizes, (dx, dy, 0))
            edge = v[15 if dx > 0 else 0, (15 if dy > 0 else 0) : (16 if dy > 0 else 1), :]

            put_row(msg, peer, ok, edge)

    for step in ((-1, 0), (1, 0), (0, -1), (0, 1)):
        for dz in (-1, 1):
            peer, ok = neighbour(pos_ref, sizes, (*step, dz))
            edge = marks[3:4] if dz > 0 else marks[0:1]

            put_row(msg, peer, ok, edge)


def heads(pos_ref, sizes, got, step):
    row, ok = neighbour(pos_ref, sizes, step)
    return take_row(got, row, ok, slice(0, 128))


def entry(head, tile, which):
    lane = HEAD + 7 * tile + which
    return head[:, lane : lane + 1]


def edges_of(pos_ref, sizes, got, step):
    row, ok = neighbour(pos_ref, sizes, step)
    return take_row(got, row, ok, slice(128, 256))


def tile_planes(pos_ref, sizes, got1, cx, cy, cz):
    own = heads(pos_ref, sizes, got1, (0, 0, 0))
    ends = {s: heads(pos_ref, sizes, got1, s) for s in ((-1, 0, 0), (1, 0, 0), (0, -1, 0), (0, 1, 0), (0, 0, -1), (0, 0, 1))}
    for k, (head, tile) in enumerate(((ends[-1, 0, 0], 1), (own, 0), (own, 1), (ends[1, 0, 0], 0))):
        for n, which in enumerate((0, 3, 4)):
            cx[k, n] = jnp.broadcast_to(entry(head, tile, which), (16, 128))
    rows, lanes = iota((32, 128), 0), iota((16, 256), 1)
    for tile in range(2):
        for n, which in enumerate((3, 1, 5)):
            cy[tile, n] = jnp.where(
                rows == 7,
                entry(ends[0, -1, 0], tile, which),
                jnp.where(rows == 24, entry(ends[0, 1, 0], tile, which), entry(own, tile, which)),
            )
        for n, which in enumerate((4, 5, 2)):
            cz[tile, n] = jnp.where(
                lanes == 255,
                entry(ends[0, 0, -1], tile, which),
                jnp.where(lanes == 128, entry(ends[0, 0, 1], tile, which), entry(own, tile, which)),
            )
    return entry(own, 0, 6), entry(own, 1, 6)


def fill_extended(vext, v, faces, got, pos_ref, sizes):
    xm, xp, ym, yp, zm, zp = faces
    vext[2:18, 8:24, 0:128] = v[...]
    vext[0:2, 8:24, 0:128] = xm[...]
    vext[18:20, 8:24, 0:128] = xp[...]
    vext[2:18, 0:8, 0:128] = ym[...]
    vext[2:18, 24:32, 0:128] = yp[...]
    row, lane = iota((8, 128), 0), iota((8, 128), 1)
    place = ((row < 4) & (lane == jnp.where(row < 2, row + 126, row - 2))).astype(F32)
    outer = jnp.concatenate([zm[...], zp[...], jnp.zeros((4, 256), F32)], 0)
    beyond = lax.dot_general(outer, place, TN, precision=HIGHEST, preferred_element_type=F32)
    vext[2:18, 8:24, 128:256] = beyond.reshape(16, 16, 128)
    for dx, i in ((-1, 1), (1, 18)):
        for dy, j in ((-1, 7), (1, 24)):
            vext[i, j : j + 1, 0:128] = edges_of(pos_ref, sizes, got, (dx, dy, 0))
    lanes = iota((1, 128), 1)
    group = lanes // 16
    lines = []
    for dz in (-1, 1):
        line = jnp.zeros((1, 128), F32)
        for g, (dx, dy) in enumerate(((1, 0), (-1, 0), (0, 1), (0, -1))):
            line = jnp.where(group == g, edges_of(pos_ref, sizes, got, (dx, dy, dz)), line)
        lines.append(line)
    outer = jnp.concatenate([*lines, jnp.zeros((6, 128), F32)], 0)
    place = ((row < 2) & (lane == jnp.where(row == 0, 127, 0))).astype(F32)
    beyond = lax.dot_general(outer, place, TN, precision=HIGHEST, preferred_element_type=F32)
    vext[18, 8:24, 128:256] = beyond[0:16]
    vext[1, 8:24, 128:256] = beyond[16:32]
    for x in range(CX):
        vext[2 + x, 24:25, 128:256] = beyond[32 + x : 33 + x]
        vext[2 + x, 7:8, 128:256] = beyond[48 + x : 49 + x]


def flux_x(vext, fx, cx):
    def one(p, tile):
        wide = vext[p, 8:24, :]
        gx = vext[p + 1, 8:24, 0:128] - vext[p - 1, 8:24, 0:128]
        gy = vext[p, 9:25, 0:128] - vext[p, 7:23, 0:128]
        gz = (pltpu.roll(wide, 255, 1) - pltpu.roll(wide, 1, 1))[:, 0:128]
        fx[p - 1] = cx[tile, 0] * gx + cx[tile, 1] * gy + cx[tile, 2] * gz

    one(1, 0)
    one(18, 3)

    @pl.loop(2, 18, unroll=4)
    def _(p):
        one(p, jnp.where(p < 10, 1, 2))


def lap_plane(vext, fx, cy, cz, x):
    p = x + 2
    tile = x // 8
    wide = vext[p]
    gx = vext[p + 1] - vext[p - 1]
    gy = pltpu.roll(wide, 31, 0) - pltpu.roll(wide, 1, 0)
    gz = pltpu.roll(wide, 255, 1) - pltpu.roll(wide, 1, 1)
    fy = cy[tile, 0] * gx[:, 0:128] + cy[tile, 1] * gy[:, 0:128] + cy[tile, 2] * gz[:, 0:128]
    dy = (pltpu.roll(fy, 31, 0) - pltpu.roll(fy, 1, 0))[8:24]
    fz = cz[tile, 0] * gx[8:24] + cz[tile, 1] * gy[8:24] + cz[tile, 2] * gz[8:24]
    dz = (pltpu.roll(fz, 255, 1) - pltpu.roll(fz, 1, 1))[:, 0:128]
    return 0.25 * (fx[x + 2] - fx[x] + dy + dz)


def column_wide(values):
    return jnp.concatenate([jnp.broadcast_to(values[:, z : z + 1], (64, 256)) for z in range(4)], 0)


def to_row(wide):
    return jnp.sum(jnp.where(iota((256, 256), 0) == iota((256, 256), 1), wide, 0.0), axis=0, keepdims=True)


def first_kernel(sizes, pos_ref, act_ref, fi_ref, half_ref, slope_ref, tau_ref, cond_ref, rev_ref, angle, conduct, block_elem,
                 states, s1, xlo, xhi, ylo, yhi, zlo, zhi, msg, code_col, code_row, const, lines):
    gate_constants(half_ref, slope_ref, tau_ref, cond_ref, rev_ref, const)

    @pl.loop(0, CX)
    def _(x):
        alive = act_ref[x // 8, 0, 0] > 0
        s1[0, x] = ionic_plane(states[0, x], states, s1, x, alive, const)[0]

    ids = block_elem[...].reshape(64, 4)
    owner = column_wide((ids // ELEMS).astype(F32))
    local = column_wide((ids % ELEMS).astype(F32))
    owner_row = to_row(owner)
    before = iota((256, 256), 1) < iota((256, 256), 0)
    rank = jnp.sum(jnp.where((owner == owner_row) & before, 1.0, 0.0), axis=1, keepdims=True)
    code = owner + 256.0 * rank
    code_col[...] = code[:, 0:128]
    row_code = to_row(code)
    code_row[...] = jnp.broadcast_to(row_code, (8, 256))
    local_row = to_row(local) + 1.0
    peers = iota((256, 256), 0).astype(F32)
    lane = iota((1, 128), 1)
    a, b = frame_of(angle), conduct[...]
    spread = b[0:1] - b[1:2]
    entries = [b[1:2] + spread * a[n] * a[n] for n in range(3)]
    entries += [spread * a[0] * a[1], spread * a[0] * a[2], spread * a[1] * a[2]]
    head = jnp.zeros((1, 128), F32)
    slots = iota((1, NF), 1)
    for tile in range(2):
        alive = (act_ref[tile, 0, 0] > 0).astype(F32)
        chosen = slots == fi_ref[tile, 0, 0]
        for n in range(6):
            value = jnp.sum(jnp.where(chosen, entries[n], 0.0), axis=1, keepdims=True) * alive
            head = jnp.where(lane == HEAD + 7 * tile + n, value, head)
        head = jnp.where(lane == HEAD + 7 * tile + 6, alive, head)
    asked = jnp.broadcast_to(head, (256, 128))
    target = iota((128, 256), 0)
    for r in range(2):
        goes = (row_code == peers + 256.0 * r).astype(F32).astype(BF16)
        labels = jnp.where(target == r, local_row, 0.0).astype(BF16)
        asked += lax.dot_general(goes, labels, NT, preferred_element_type=F32)
    msg[:, 0:128] = asked
    msg[:, 128:256] = jnp.zeros((256, 128), F32)
    send_faces(s1.at[0], pos_ref, sizes, xlo, xhi, ylo, yhi, zlo, zhi, msg, lines)


def element_kernel(material, angle, node_disp, elem_node, elem_fibre, corner, passive, active):
    table = jnp.concatenate([*frame_of(angle), jnp.zeros((5, NF), F32)], 0)
    hot = (iota((NF, ELEMS), 0) == elem_fibre[...]).astype(F32)
    fibre = jnp.dot(table, hot, precision=HIGHEST, preferred_element_type=F32)
    f = [fibre[j : j + 1] for j in range(3)]
    disp = jnp.concatenate([node_disp[...], jnp.zeros((5, NODES), F32)], 0)
    packed = jnp.concatenate([p.astype(F32) for p in parts3(disp)] + [jnp.zeros((8, NODES), F32)], 0).astype(BF16)
    slope = [jnp.zeros((8, ELEMS), F32) for _ in range(3)]
    for q in range(8):
        hot = (iota((NODES, ELEMS), 0) == elem_node[q : q + 1, :]).astype(F32).astype(BF16)
        got = jnp.dot(packed, hot, preferred_element_type=F32)
        got = got[0:8] + got[8:16] + got[16:24]
        corner[8 * q : 8 * q + 8] = got
        for j in range(3):
            slope[j] += got if CORNERS[q][j] else -got
    F = [[slope[j][i : i + 1] * 0.25 + (1.0 if i == j else 0.0) for j in range(3)] for i in range(3)]

    def cofactor(i, j):
        a, b = [n for n in range(3) if n != i]
        c, d = [n for n in range(3) if n != j]
        minor = F[a][c] * F[b][d] - F[a][d] * F[b][c]
        return minor if (i + j) % 2 == 0 else -minor

    cof = [[cofactor(i, j) for j in range(3)] for i in range(3)]
    volume = F[0][0] * cof[0][0] + F[0][1] * cof[0][1] + F[0][2] * cof[0][2]
    invert = 1.0 / volume
    bulk = material[1] * jnp.log(volume)
    none = jnp.zeros((5, ELEMS), F32)
    stress, fibres = [], []
    stretch = [F[i][0] * f[0] + F[i][1] * f[1] + F[i][2] * f[2] for i in range(3)]
    for j in range(3):
        rows = []
        for i in range(3):
            inverse = cof[i][j] * invert
            rows.append(material[0] * (F[i][j] - inverse) + bulk * inverse)
        stress.append(jnp.concatenate([*rows, none], 0))
        fibres.append(jnp.concatenate([*[material[2] * stretch[i] * f[j] for i in range(3)], none], 0))
    total = jnp.zeros((24, NODES), F32)
    for q in range(8):
        sign = [0.25 if CORNERS[q][j] else -0.25 for j in range(3)]
        force = stress[0] * sign[0] + stress[1] * sign[1] + stress[2] * sign[2]
        active[8 * q : 8 * q + 8] = fibres[0] * sign[0] + fibres[1] * sign[1] + fibres[2] * sign[2]
        hot = (iota((NODES, ELEMS), 0) == elem_node[q : q + 1, :]).astype(F32).astype(BF16)
        packed = jnp.concatenate([p.astype(F32) for p in parts3(force)], 0).astype(BF16)
        total += lax.dot_general(packed, hot, NT, preferred_element_type=F32)
    passive[...] = total[0:8] + total[8:16] + total[16:24]


def second_kernel(sizes, pos_ref, half_ref, slope_ref, tau_ref, cond_ref, rev_ref, s1, xm, xp, ym, yp, zm, zp, got1, corner,
                  code_row, block_weight, s2, xlo, xhi, ylo, yhi, zlo, zhi, msg, const, lines, vext, fx, cx, cy, cz, tens):
    gate_constants(half_ref, slope_ref, tau_ref, cond_ref, rev_ref, const)
    live = tile_planes(pos_ref, sizes, got1, cx, cy, cz)
    fill_extended(vext, s1.at[0], (xm, xp, ym, yp, zm, zp), got1, pos_ref, sizes)
    flux_x(vext, fx, cx)

    @pl.loop(0, CX)
    def _(x):
        here = jnp.where(x < 8, live[0], live[1])
        volt = s1[0, x] + here * lap_plane(vext, fx, cy, cz, x)
        alive = jnp.broadcast_to(here, (16, 128)) > 0.5
        vstar, calcium = ionic_plane(volt, s1, s2, x, alive, const)
        s2[0, x] = vstar
        square = calcium * calcium
        tens[x] = square / (square + 0.09)

    pairs = jnp.concatenate([tens[2 * n] + tens[2 * n + 1] for n in range(8)], 0)
    row, lane = iota((64, 128), 0), iota((64, 128), 1)
    over_y = ((row // 8 == lane // 16) & (row % 8 == lane % 16 // 2)).astype(F32)
    over_z = jnp.where(iota((128, 128), 0) // 32 == iota((128, 128), 1), 1.0 / 128.0, 0.0)
    mean = jnp.dot(over_y, pairs, precision=HIGHEST, preferred_element_type=F32)
    mean = jnp.dot(mean, over_z, precision=HIGHEST, preferred_element_type=F32)
    value = to_row(column_wide(mean[:, 0:4] * block_weight[...].reshape(64, 4)))
    peers = iota((256, 256), 0).astype(F32)
    elems = iota((256, 256), 1).astype(F32)
    target = iota((128, 256), 0)
    answer = jnp.zeros((256, 128), F32)
    none = jnp.zeros((64, 256), F32)
    for r in range(2):
        goes = (code_row[0:1, :] == peers + 256.0 * r).astype(F32).astype(BF16)
        for part in parts3(jnp.where(target == 64 * r + 3, value, 0.0)):
            answer += lax.dot_general(goes, part, NT, preferred_element_type=F32)
        wants = (got1[:, r : r + 1] == elems + 1.0).astype(F32).astype(BF16)
        held = jnp.concatenate([corner[...], none] if r == 0 else [none, corner[...]], 0)
        for part in parts3(held):
            answer += lax.dot_general(wants, part, NT, preferred_element_type=F32)
    msg[:, 0:128] = answer
    msg[:, 128:256] = jnp.zeros((256, 128), F32)
    send_faces(s2.at[0], pos_ref, sizes, xlo, xhi, ylo, yhi, zlo, zhi, msg, lines)


def third_kernel(sizes, pos_ref, s2, xm, xp, ym, yp, zm, zp, got1, got2, code_col, elem_node, passive, active, blend, s3, fine,
                 residual, vext, fx, cx, cy, cz):
    live = tile_planes(pos_ref, sizes, got1, cx, cy, cz)
    fill_extended(vext, s2.at[0], (xm, xp, ym, yp, zm, zp), got2, pos_ref, sizes)
    flux_x(vext, fx, cx)

    @pl.loop(0, CX)
    def _(x):
        here = jnp.where(x < 8, live[0], live[1])
        s3[0, x] = s2[0, x] + here * lap_plane(vext, fx, cy, cz, x)

    elems = iota((256, 256), 1).astype(F32)
    tension = jnp.zeros((1, 256), F32)
    for r in range(2):
        wants = got1[:, r : r + 1] == elems + 1.0
        tension += jnp.sum(jnp.where(wants, got2[:, 64 * r + 3 : 64 * r + 4], 0.0), axis=0, keepdims=True)
    total = jnp.zeros((24, NODES), F32)
    for q in range(8):
        hot = (iota((NODES, ELEMS), 0) == elem_node[q : q + 1, :]).astype(F32).astype(BF16)
        packed = jnp.concatenate([p.astype(F32) for p in parts3(active[8 * q : 8 * q + 8] * tension)], 0).astype(BF16)
        total += lax.dot_general(packed, hot, NT, preferred_element_type=F32)
    total = passive[...] + total[0:8] + total[8:16] + total[16:24]
    residual[...] = total[0:3]

    code = jnp.concatenate([code_col[...], code_col[...]], 1)
    answer = got2[:, 0:128]
    lane = iota((256, 128), 1)
    disp = jnp.zeros((256, 128), F32)
    for r in range(2):
        goes = (code == elems + 256.0 * r).astype(F32).astype(BF16)
        part = jnp.where(lane // 64 == r, answer, 0.0)
        part = part if r == 0 else pltpu.roll(part, 64, 1)
        for piece in parts3(part):
            disp += jnp.dot(goes, piece, preferred_element_type=F32)
    merged = jnp.concatenate(
        [disp[0:64] + pltpu.roll(disp[64:128], 64, 1), disp[128:192] + pltpu.roll(disp[192:256], 64, 1)], 1
    )
    which = iota((64, 256), 1) % 8
    rows = jnp.concatenate([jnp.where(which == c, merged, 0.0) for c in range(3)], 0)
    first, second, third = parts3(rows)
    out = jnp.dot(first, blend[0], preferred_element_type=F32) + jnp.dot(second, blend[0], preferred_element_type=F32)
    out += jnp.dot(first, blend[1], preferred_element_type=F32)
    for c in range(3):
        for bx in range(8):
            tile = out[64 * c + 8 * bx : 64 * c + 8 * bx + 8]
            for i in range(2):
                for j in range(2):
                    at = 128 * (2 * i + j)
                    fine[c, 2 * bx + i, pl.ds(j, 8, stride=2), :] = tile[:, at : at + 128]


def blend_table():
    table = np.zeros((4, 8, 8, 2, 2, 128), np.float64)
    z = np.arange(128)
    for q, bits in enumerate(CORNERS):
        for i in range(2):
            for j in range(2):
                for bz in range(4):
                    xi = ((i + 0.5) / 2, (j + 0.5) / 2, (z % 32 + 0.5) / 32)
                    w = 1.0
                    for d in range(3):
                        w = w * (xi[d] if bits[d] else 1.0 - xi[d])
                    table[bz, q, :, i, j] = w * (z // 32 == bz)
    table = table.reshape(256, 512)
    import ml_dtypes

    first = table.astype(ml_dtypes.bfloat16)
    second = (table - first.astype(np.float64)).astype(ml_dtypes.bfloat16)
    return np.stack([first, second])


def shift(x, axis, by):
    count = lax.axis_size(axis)
    pairs = [(i, i + by) for i in range(count) if 0 <= i + by < count]
    return lax.ppermute(x, axis, pairs)


def exchange(xlo, xhi, ylo, yhi, zlo, zhi, msg):
    got = lax.all_to_all(msg.reshape(256, 1, 256), ALL, 0, 0, tiled=True).reshape(256, 256)
    return (
        shift(xhi, "gx", 1),
        shift(xlo, "gx", -1),
        shift(yhi, "gy", 1),
        shift(ylo, "gy", -1),
        shift(zhi, "gz", 1),
        shift(zlo, "gz", -1),
    ), got


SMEM = pl.BlockSpec(memory_space=pltpu.SMEM)
VMEM = pl.BlockSpec(memory_space=pltpu.VMEM)


def sds(*shape):
    return jax.ShapeDtypeStruct(shape, F32)


FACES = [sds(2, 16, 128), sds(2, 16, 128), sds(16, 8, 128), sds(16, 8, 128), sds(2, 256), sds(2, 256), sds(256, 256)]
STEP_SCRATCH = [
    pltpu.VMEM((20, 32, 256), F32),
    pltpu.VMEM((18, 16, 128), F32),
    pltpu.VMEM((4, 3, 16, 128), F32),
    pltpu.VMEM((2, 3, 32, 128), F32),
    pltpu.VMEM((2, 3, 16, 256), F32),
]
GATE_SCRATCH = [pltpu.VMEM((6 * NCH, 8, 128), F32), pltpu.VMEM((128, 128), F32)]
PARAMS = pltpu.CompilerParams(vmem_limit_bytes=40 * 2**20)


def shards(states, active, fibre_index, fibre_angle, conduct, gate_half, gate_slope, gate_tau, conductance, reversal,
           block_elem, block_weight, node_disp, elem_node, elem_fibre, material):
    sizes = tuple(lax.axis_size(a) for a in ALL)
    pos = jnp.stack([lax.axis_index(a) for a in ALL]).astype(jnp.int32)
    gates = (gate_half, gate_slope, gate_tau, conductance, reversal)
    full = sds(NSTATE, CX, CY, CZ)
    s1, *faces, code_col, code_row = pl.pallas_call(
        functools.partial(first_kernel, sizes),
        out_shape=[full, *FACES, sds(256, 128), sds(8, 256)],
        in_specs=[SMEM] * 8 + [VMEM] * 4,
        out_specs=[VMEM] * 10,
        scratch_shapes=GATE_SCRATCH,
        compiler_params=PARAMS,
        name="first",
    )(pos, active, fibre_index, *gates, fibre_angle, conduct, block_elem, states)
    halo, got1 = exchange(*faces)
    corner, passive, active_force = pl.pallas_call(
        element_kernel,
        out_shape=[sds(64, ELEMS), sds(8, NODES), sds(64, ELEMS)],
        in_specs=[SMEM] + [VMEM] * 4,
        out_specs=[VMEM] * 3,
        compiler_params=PARAMS,
        name="elements",
    )(material, fibre_angle, node_disp, elem_node, elem_fibre.reshape(1, ELEMS))
    s2, *faces = pl.pallas_call(
        functools.partial(second_kernel, sizes),
        out_shape=[full, *FACES],
        in_specs=[SMEM] * 6 + [VMEM] * 11,
        out_specs=[VMEM] * 8,
        scratch_shapes=GATE_SCRATCH + STEP_SCRATCH + [pltpu.VMEM((16, 16, 128), F32)],
        compiler_params=PARAMS,
        name="second",
    )(pos, *gates, s1, *halo, got1, corner, code_row, block_weight)
    halo, got2 = exchange(*faces)
    plane = pl.BlockSpec((1, CX, CY, CZ), lambda i: (0, 0, 0, 0))

    def whole(x):
        return pl.BlockSpec(x.shape, lambda i: (0,) * x.ndim)

    blend = jnp.asarray(blend_table())
    rest = (*halo, got1, got2, code_col, elem_node, passive, active_force, blend)
    outs = [full, sds(3, CX, CY, CZ), sds(3, NODES)]
    return pl.pallas_call(
        functools.partial(third_kernel, sizes),
        grid=(1,),
        out_shape=outs,
        in_specs=[SMEM, plane, *[whole(x) for x in rest]],
        out_specs=[plane, whole(outs[1]), whole(outs[2])],
        scratch_shapes=STEP_SCRATCH,
        input_output_aliases={1: 0},
        compiler_params=PARAMS,
        name="third",
    )(pos, s2, *rest)


def solution(mesh):
    in_specs = (
        P(None, "gx", "gy", "gz"),
        *[P("gx", "gy", "gz")] * 2,
        *[P()] * 7,
        *[P("gx", "gy", "gz")] * 2,
        *[P(None, ALL)] * 2,
        P(ALL),
        P(),
    )
    out_specs = (P(None, "gx", "gy", "gz"), P(None, "gx", "gy", "gz"), P(None, ALL))
    return jax.shard_map(shards, mesh=mesh, in_specs=in_specs, out_specs=out_specs, check_vma=False)
```

profile of v0, /device:TPU:75, one launch (start us, length us, event | category | flops | bytes accessed | tf_op | source)
XLA Modules:
  0.0 121.7 jit_solution(10829255119418574499)
XLA Ops:
  3.1 1.7 %copy-done = f32[19,16,16,128]{3,2,1,0:T(8,128)S(1)} copy-done((f32[19,16,16,128]{3,2,1,0:T(8,128)S(1)}, f32[19,16,16,128]{3,2,1,0:T(8,128)}, u32[]{:S(2)}) %copy-start) | copy-done | bytes 2490392
  9.4 3.2 %first.1 = (f32[19,16,16,128]{3,2,1,0:T(8,128)S(1)}, f32[2,16,128]{2,1,0:T(8,128)}, f32[2,16,128]{2,1,0:T(8,128)}, f32[16,8,128]{2,1,0:T(8,128)}, f32[16,8,128]{...) custom-call(s32[3]{0:T(128)S(1)} %pad_add_fusion.pos_ref, ...), custom_call_target="tpu_custom_call" | custom-call | tf_op jit(solution)/shard_map/first/pallas_call | solution.py:490
  12.6 1.0 copy.28
  13.6 15.5 %all-to-all-start = ((f32[256,1,256]{2,1,0:T(1,128)}), f32[256,1,256]{2,1,0:T(1,128)}, u32[]{:S(2)}, u32[]{:S(2)}) async-start(f32[256,1,256]{2,1,0:T(1,128)} %copy.28), calls=%async_computation | async-start | bytes 524288 | tf_op jit(solution)/shard_map/all_to_all | solution.py:453
  29.1 3.2 %collective-permute-start.2 = (f32[16,8,128]{2,1,0:T(8,128)}, f32[16,8,128]{2,1,0:T(8,128)}, u32[]{:S(2)}, u32[]{:S(2)}) collective-permute-start(f32[16,8,128]{2,1,0:T(8,128)} %get-tuple-element.27), channel_id=1, source_target_pairs={{0,8},{8,16},{16,24},{1,9},{9,17},{17,25},{2,10},{10,18},{18,26},{... | collective-permute-start | bytes 196616 | tf_op jit(solution)/shard_map/ppermute | solution.py:449
  32.2 2.7 %collective-permute-start.3 = (f32[16,8,128]{2,1,0:T(8,128)}, f32[16,8,128]{2,1,0:T(8,128)}, u32[]{:S(2)}, u32[]{:S(2)}) collective-permute-start(f32[16,8,128]{2,1,0:T(8,128)} %get-tuple-element.28), channel_id=1, source_target_pairs={{8,0},{16,8},{24,16},{9,1},{17,9},{25,17},{10,2},{18,10},{26,18},{... | collective-permute-start | bytes 196616 | tf_op jit(solution)/shard_map/ppermute | solution.py:449
  35.0 3.4 %collective-permute-start = (f32[2,16,128]{2,1,0:T(8,128)}, f32[2,16,128]{2,1,0:T(8,128)S(1)}, u32[]{:S(2)}, u32[]{:S(2)}) collective-permute-start(f32[2,16,128]{2,1,0:T(8,128)} %get-tuple-element.25), channel_id=1, source_target_pairs={{0,32},{32,64},{64,96},{96,128},{128,160},{160,192},{192,224},{1,3... | collective-permute-start | bytes 49160 | tf_op jit(solution)/shard_map/ppermute | solution.py:449
  38.3 2.8 %collective-permute-start.1 = (f32[2,16,128]{2,1,0:T(8,128)}, f32[2,16,128]{2,1,0:T(8,128)}, u32[]{:S(2)}, u32[]{:S(2)}) collective-permute-start(f32[2,16,128]{2,1,0:T(8,128)} %get-tuple-element.26), channel_id=1, source_target_pairs={{32,0},{64,32},{96,64},{128,96},{160,128},{192,160},{224,192},{33,... | collective-permute-start | bytes 49160 | tf_op jit(solution)/shard_map/ppermute | solution.py:449
  41.2 7.1 %collective-permute-start.4 = (f32[2,256]{1,0:T(2,128)S(1)}, f32[2,256]{1,0:T(2,128)S(1)}, u32[]{:S(2)}, u32[]{:S(2)}) collective-permute-start(f32[2,256]{1,0:T(2,128)S(1)} %get-tuple-element.29), channel_id=1, source_target_pairs={{0,1},{1,2},{2,3},{3,4},{4,5},{5,6},{6,7},{8,9},{9,10},{10,11},{11... | collective-permute-start | bytes 6152 | tf_op jit(solution)/shard_map/ppermute | solution.py:449
  49.0 1.9 %collective-permute-start.5 = (f32[2,256]{1,0:T(2,128)}, f32[2,256]{1,0:T(2,128)}, u32[]{:S(2)}, u32[]{:S(2)}) collective-permute-start(f32[2,256]{1,0:T(2,128)} %get-tuple-element.30), channel_id=1, source_target_pairs={{1,0},{2,1},{3,2},{4,3},{5,4},{6,5},{7,6},{9,8},{10,9},{11,10},{12... | collective-permute-start | bytes 6152 | tf_op jit(solution)/shard_map/ppermute | solution.py:449
  51.1 1.8 %elements.1 = (f32[64,256]{1,0:T(8,128)S(1)}, f32[8,512]{1,0:T(8,128)S(1)}, f32[64,256]{1,0:T(8,128)S(1)}) custom-call(f32[3]{0:T(128)S(1)} %copy-done.25, f32[2,64]{1,0:T(2,128)S(1)} %copy-done.10, f32[3,512]{1,0:T(4,128)S(1)} %copy-done.5, s32[8,256]{1,0:T(8,128)S(1)} %copy-done.4, s32[1,256]{1,0:T(1,128)S(1)} %bitcast.17), custom_call_target="tpu_custom_call" | custom-call | tf_op jit(solution)/shard_map/elements/pallas_call | solution.py:500
  53.5 1.0 copy.36
  54.5 2.3 %collective-permute-done.5.zp = f32[2,256]{1,0:T(2,128)} collective-permute-done((f32[2,256]{1,0:T(2,128)}, f32[2,256]{1,0:T(2,128)}, u32[]{:S(2)}, u32[]{:S(2)}) %collective-permute-start.5) | collective-permute-done | bytes 2080 | tf_op jit(solution)/shard_map/ppermute | solution.py:449
  62.3 8.5 %second.1 = (f32[19,16,16,128]{3,2,1,0:T(8,128)}, f32[2,16,128]{2,1,0:T(8,128)S(1)}, f32[2,16,128]{2,1,0:T(8,128)S(1)}, f32[16,8,128]{2,1,0:T(8,128)S(1)}, f32[1...) custom-call(s32[3]{0:T(128)S(1)} %copy-done.7, f32[17]{0:T(128)S(1)} %copy-done.14, ...), custom_call_target="tpu_custom_call" | custom-call | tf_op jit(solution)/shard_map/second/pallas_call | solution.py:508
  74.4 1.0 copy.30
  75.4 11.6 %all-to-all-start.1 = ((f32[256,1,256]{2,1,0:T(1,128)}), f32[256,1,256]{2,1,0:T(1,128)S(1)}, u32[]{:S(2)}, u32[]{:S(2)}) async-start(f32[256,1,256]{2,1,0:T(1,128)} %copy.30), calls=%async_computation.1 | async-start | bytes 524288 | tf_op jit(solution)/shard_map/all_to_all | solution.py:453
  87.0 3.2 %collective-permute-start.8 = (f32[16,8,128]{2,1,0:T(8,128)}, f32[16,8,128]{2,1,0:T(8,128)S(1)}, u32[]{:S(2)}, u32[]{:S(2)}) collective-permute-start(f32[16,8,128]{2,1,0:T(8,128)} %copy-done.27), channel_id=1, source_target_pairs={{0,8},{8,16},{16,24},{1,9},{9,17},{17,25},{2,10},{10,18},{18,26},{... | collective-permute-start | bytes 196616 | tf_op jit(solution)/shard_map/ppermute | solution.py:449
  90.2 2.1 %collective-permute-start.9 = (f32[16,8,128]{2,1,0:T(8,128)}, f32[16,8,128]{2,1,0:T(8,128)S(1)}, u32[]{:S(2)}, u32[]{:S(2)}) collective-permute-start(f32[16,8,128]{2,1,0:T(8,128)} %copy-done.26), channel_id=1, source_target_pairs={{8,0},{16,8},{24,16},{9,1},{17,9},{25,17},{10,2},{18,10},{26,18},{... | collective-permute-start | bytes 196616 | tf_op jit(solution)/shard_map/ppermute | solution.py:449
  92.3 3.4 %collective-permute-start.6 = (f32[2,16,128]{2,1,0:T(8,128)}, f32[2,16,128]{2,1,0:T(8,128)S(1)}, u32[]{:S(2)}, u32[]{:S(2)}) collective-permute-start(f32[2,16,128]{2,1,0:T(8,128)} %copy-done.29), channel_id=1, source_target_pairs={{0,32},{32,64},{64,96},{96,128},{128,160},{160,192},{192,224},{1,3... | collective-permute-start | bytes 49160 | tf_op jit(solution)/shard_map/ppermute | solution.py:449
  95.7 2.8 %collective-permute-start.7 = (f32[2,16,128]{2,1,0:T(8,128)}, f32[2,16,128]{2,1,0:T(8,128)S(1)}, u32[]{:S(2)}, u32[]{:S(2)}) collective-permute-start(f32[2,16,128]{2,1,0:T(8,128)} %copy-done.28), channel_id=1, source_target_pairs={{32,0},{64,32},{96,64},{128,96},{160,128},{192,160},{224,192},{33,... | collective-permute-start | bytes 49160 | tf_op jit(solution)/shard_map/ppermute | solution.py:449
  98.5 7.1 %collective-permute-start.10 = (f32[2,256]{1,0:T(2,128)}, f32[2,256]{1,0:T(2,128)S(1)}, u32[]{:S(2)}, u32[]{:S(2)}) collective-permute-start(f32[2,256]{1,0:T(2,128)} %copy-done.31), channel_id=1, source_target_pairs={{0,1},{1,2},{2,3},{3,4},{4,5},{5,6},{6,7},{8,9},{9,10},{10,11},{11... | collective-permute-start | bytes 6152 | tf_op jit(solution)/shard_map/ppermute | solution.py:449
  106.5 1.9 %collective-permute-start.11 = (f32[2,256]{1,0:T(2,128)}, f32[2,256]{1,0:T(2,128)S(1)}, u32[]{:S(2)}, u32[]{:S(2)}) collective-permute-start(f32[2,256]{1,0:T(2,128)} %copy-done.30), channel_id=1, source_target_pairs={{1,0},{2,1},{3,2},{4,3},{5,4},{6,5},{7,6},{9,8},{10,9},{11,10},{12... | collective-permute-start | bytes 6152 | tf_op jit(solution)/shard_map/ppermute | solution.py:449
  108.5 5.8 %collective-permute-done.11.zp = f32[2,256]{1,0:T(2,128)S(1)} collective-permute-done((f32[2,256]{1,0:T(2,128)}, f32[2,256]{1,0:T(2,128)S(1)}, u32[]{:S(2)}, u32[]{:S(2)}) %collective-permute-start.11) | collective-permute-done | bytes 2080 | tf_op jit(solution)/shard_map/ppermute | solution.py:449
  115.0 6.7 %third.1 = (f32[19,16,16,128]{3,2,1,0:T(8,128)}, f32[3,16,16,128]{3,2,1,0:T(8,128)}, f32[3,512]{1,0:T(4,128)}) custom-call(s32[3]{0:T(128)S(1)} %copy-done.8, f32[19,16,16,128]{3,2,1,0:T(8,128)} %get-tuple-element.34.s2, f32[2,16,128]{2,1,0:T(8,128)S(1)} %collective-permute-done.6.xm, ...), custom_call_target="tpu_custom_call", output_to_operand_aliasing={{0}: (1, {})} | custom-call | tf_op jit(solution)/shard_map/third/pallas_call | solution.py:526
  (83 shorter events, 19.2 us)
Async XLA Ops:
  0.6 50.4 %copy-start.10 = (f32[2,64]{1,0:T(2,128)S(1)}, f32[2,64]{1,0:T(2,128)}, u32[]{:S(2)}) copy-start(f32[2,64]{1,0:T(2,128)} %angle.3) | copy-start | bytes 1540
  0.6 50.3 %copy-start.32 = (f32[8,8,4]{1,2,0:T(4,128)S(1)}, f32[8,8,4]{1,2,0:T(4,128)}, u32[]{:S(2)}) copy-start(f32[8,8,4]{1,2,0:T(4,128)} %param.28) | copy-start | bytes 3076
  0.7 50.4 %copy-start.4 = (s32[8,256]{1,0:T(8,128)S(1)}, s32[8,256]{1,0:T(8,128)}, u32[]{:S(2)}) copy-start(s32[8,256]{1,0:T(8,128)} %elem_node.3) | copy-start | bytes 24580
  0.7 50.4 %copy-start.25 = (f32[3]{0:T(128)S(1)}, f32[3]{0:T(128)}, u32[]{:S(2)}) copy-start(f32[3]{0:T(128)} %material.1) | copy-start | bytes 40
  0.7 50.4 %copy-start.24 = (s32[256]{0:T(256)S(1)}, s32[256]{0:T(256)}, u32[]{:S(2)}) copy-start(s32[256]{0:T(256)} %param.31) | copy-start | bytes 3076
  0.7 50.4 %copy-start.5 = (f32[3,512]{1,0:T(4,128)S(1)}, f32[3,512]{1,0:T(4,128)}, u32[]{:S(2)}) copy-start(f32[3,512]{1,0:T(4,128)} %node_disp.1) | copy-start | bytes 18436
  3.1 1.7 %copy-start = (f32[19,16,16,128]{3,2,1,0:T(8,128)S(1)}, f32[19,16,16,128]{3,2,1,0:T(8,128)}, u32[]{:S(2)}) copy-start(f32[19,16,16,128]{3,2,1,0:T(8,128)} %states.1) | copy-start | bytes 7471108
  9.4 3.2 %copy-start.6 = (s32[3]{0:T(128)}, s32[3]{0:T(128)S(1)}, u32[]{:S(2)}) copy-start(s32[3]{0:T(128)S(1)} %pad_add_fusion.pos_ref) | copy-start | bytes 40
  13.6 39.9 %all-to-all-start = ((f32[256,1,256]{2,1,0:T(1,128)}), f32[256,1,256]{2,1,0:T(1,128)}, u32[]{:S(2)}, u32[]{:S(2)}) async-start(f32[256,1,256]{2,1,0:T(1,128)} %copy.28), calls=%async_computation | async-start | bytes 524288 | tf_op jit(solution)/shard_map/all_to_all | solution.py:453
  29.1 27.8 %collective-permute-start.2 = (f32[16,8,128]{2,1,0:T(8,128)}, f32[16,8,128]{2,1,0:T(8,128)}, u32[]{:S(2)}, u32[]{:S(2)}) collective-permute-start(f32[16,8,128]{2,1,0:T(8,128)} %get-tuple-element.27), channel_id=1, source_target_pairs={{0,8},{8,16},{16,24},{1,9},{9,17},{17,25},{2,10},{10,18},{18,26},{... | collective-permute-start | bytes 196616 | tf_op jit(solution)/shard_map/ppermute | solution.py:449
  32.2 24.6 %collective-permute-start.3 = (f32[16,8,128]{2,1,0:T(8,128)}, f32[16,8,128]{2,1,0:T(8,128)}, u32[]{:S(2)}, u32[]{:S(2)}) collective-permute-start(f32[16,8,128]{2,1,0:T(8,128)} %get-tuple-element.28), channel_id=1, source_target_pairs={{8,0},{16,8},{24,16},{9,1},{17,9},{25,17},{10,2},{18,10},{26,18},{... | collective-permute-start | bytes 196616 | tf_op jit(solution)/shard_map/ppermute | solution.py:449
  35.0 21.9 %collective-permute-start = (f32[2,16,128]{2,1,0:T(8,128)}, f32[2,16,128]{2,1,0:T(8,128)S(1)}, u32[]{:S(2)}, u32[]{:S(2)}) collective-permute-start(f32[2,16,128]{2,1,0:T(8,128)} %get-tuple-element.25), channel_id=1, source_target_pairs={{0,32},{32,64},{64,96},{96,128},{128,160},{160,192},{192,224},{1,3... | collective-permute-start | bytes 49160 | tf_op jit(solution)/shard_map/ppermute | solution.py:449
  38.3 18.5 %collective-permute-start.1 = (f32[2,16,128]{2,1,0:T(8,128)}, f32[2,16,128]{2,1,0:T(8,128)}, u32[]{:S(2)}, u32[]{:S(2)}) collective-permute-start(f32[2,16,128]{2,1,0:T(8,128)} %get-tuple-element.26), channel_id=1, source_target_pairs={{32,0},{64,32},{96,64},{128,96},{160,128},{192,160},{224,192},{33,... | collective-permute-start | bytes 49160 | tf_op jit(solution)/shard_map/ppermute | solution.py:449
  41.2 7.8 %collective-permute-start.4 = (f32[2,256]{1,0:T(2,128)S(1)}, f32[2,256]{1,0:T(2,128)S(1)}, u32[]{:S(2)}, u32[]{:S(2)}) collective-permute-start(f32[2,256]{1,0:T(2,128)S(1)} %get-tuple-element.29), channel_id=1, source_target_pairs={{0,1},{1,2},{2,3},{3,4},{4,5},{5,6},{6,7},{8,9},{9,10},{10,11},{11... | collective-permute-start | bytes 6152 | tf_op jit(solution)/shard_map/ppermute | solution.py:449
  49.0 2.1 %copy-start.11 = (f32[2,256]{1,0:T(2,128)}, f32[2,256]{1,0:T(2,128)S(1)}, u32[]{:S(2)}) copy-start(f32[2,256]{1,0:T(2,128)S(1)} %collective-permute-done.4.zm) | copy-start | bytes 6148
  49.0 7.9 %collective-permute-start.5 = (f32[2,256]{1,0:T(2,128)}, f32[2,256]{1,0:T(2,128)}, u32[]{:S(2)}, u32[]{:S(2)}) collective-permute-start(f32[2,256]{1,0:T(2,128)} %get-tuple-element.30), channel_id=1, source_target_pairs={{1,0},{2,1},{3,2},{4,3},{5,4},{6,5},{7,6},{9,8},{10,9},{11,10},{12... | collective-permute-start | bytes 6152 | tf_op jit(solution)/shard_map/ppermute | solution.py:449
  53.5 60.8 %copy-start.1 = (bf16[2,256,512]{2,1,0:T(8,128)(2,1)S(1)}, bf16[2,256,512]{2,1,0:T(8,128)(2,1)}, u32[]{:S(2)}) copy-start(bf16[2,256,512]{2,1,0:T(8,128)(2,1)} %constant.14.clone.blend) | copy-start | bytes 1572868
  75.4 33.0 %all-to-all-start.1 = ((f32[256,1,256]{2,1,0:T(1,128)}), f32[256,1,256]{2,1,0:T(1,128)S(1)}, u32[]{:S(2)}, u32[]{:S(2)}) async-start(f32[256,1,256]{2,1,0:T(1,128)} %copy.30), calls=%async_computation.1 | async-start | bytes 524288 | tf_op jit(solution)/shard_map/all_to_all | solution.py:453
  87.0 27.3 %collective-permute-start.8 = (f32[16,8,128]{2,1,0:T(8,128)}, f32[16,8,128]{2,1,0:T(8,128)S(1)}, u32[]{:S(2)}, u32[]{:S(2)}) collective-permute-start(f32[16,8,128]{2,1,0:T(8,128)} %copy-done.27), channel_id=1, source_target_pairs={{0,8},{8,16},{16,24},{1,9},{9,17},{17,25},{2,10},{10,18},{18,26},{... | collective-permute-start | bytes 196616 | tf_op jit(solution)/shard_map/ppermute | solution.py:449
  90.2 24.1 %collective-permute-start.9 = (f32[16,8,128]{2,1,0:T(8,128)}, f32[16,8,128]{2,1,0:T(8,128)S(1)}, u32[]{:S(2)}, u32[]{:S(2)}) collective-permute-start(f32[16,8,128]{2,1,0:T(8,128)} %copy-done.26), channel_id=1, source_target_pairs={{8,0},{16,8},{24,16},{9,1},{17,9},{25,17},{10,2},{18,10},{26,18},{... | collective-permute-start | bytes 196616 | tf_op jit(solution)/shard_map/ppermute | solution.py:449
  92.3 22.0 %collective-permute-start.6 = (f32[2,16,128]{2,1,0:T(8,128)}, f32[2,16,128]{2,1,0:T(8,128)S(1)}, u32[]{:S(2)}, u32[]{:S(2)}) collective-permute-start(f32[2,16,128]{2,1,0:T(8,128)} %copy-done.29), channel_id=1, source_target_pairs={{0,32},{32,64},{64,96},{96,128},{128,160},{160,192},{192,224},{1,3... | collective-permute-start | bytes 49160 | tf_op jit(solution)/shard_map/ppermute | solution.py:449
  95.7 18.6 %collective-permute-start.7 = (f32[2,16,128]{2,1,0:T(8,128)}, f32[2,16,128]{2,1,0:T(8,128)S(1)}, u32[]{:S(2)}, u32[]{:S(2)}) collective-permute-start(f32[2,16,128]{2,1,0:T(8,128)} %copy-done.28), channel_id=1, source_target_pairs={{32,0},{64,32},{96,64},{128,96},{160,128},{192,160},{224,192},{33,... | collective-permute-start | bytes 49160 | tf_op jit(solution)/shard_map/ppermute | solution.py:449
  98.5 8.0 %collective-permute-start.10 = (f32[2,256]{1,0:T(2,128)}, f32[2,256]{1,0:T(2,128)S(1)}, u32[]{:S(2)}, u32[]{:S(2)}) collective-permute-start(f32[2,256]{1,0:T(2,128)} %copy-done.31), channel_id=1, source_target_pairs={{0,1},{1,2},{2,3},{3,4},{4,5},{5,6},{6,7},{8,9},{9,10},{10,11},{11... | collective-permute-start | bytes 6152 | tf_op jit(solution)/shard_map/ppermute | solution.py:449
  106.5 7.8 %collective-permute-start.11 = (f32[2,256]{1,0:T(2,128)}, f32[2,256]{1,0:T(2,128)S(1)}, u32[]{:S(2)}, u32[]{:S(2)}) collective-permute-start(f32[2,256]{1,0:T(2,128)} %copy-done.30), channel_id=1, source_target_pairs={{1,0},{2,1},{3,2},{4,3},{5,4},{6,5},{7,6},{9,8},{10,9},{11,10},{12... | collective-permute-start | bytes 6152 | tf_op jit(solution)/shard_map/ppermute | solution.py:449
  (23 other events, 15.0 us)
where the time goes:
time: 123 us; the launch traced here: 122 us
  starting transfers between devices  68.6 us (56%)
  local copies, waits for them, and re-layouts  22.1 us (18%)
  Pallas kernels  20.2 us (16%)
  waiting for transfers between devices  9.81 us (8%)
    ppermute x12, starting transfers between devices, shift(): return lax.ppermute(x, axis, pairs)  41.6 us
    all_to_all x2, starting transfers between devices, exchange(): lax.all_to_all(msg.reshape(256, 1, 256), ALL, 0, 0, tiled=True)  27 us
    unnamed x72, local copies, waits for them, and re-layouts  20.2 us
    ppermute x12, waiting for transfers between devices, shift(): return lax.ppermute(x, axis, pairs)  9.8 us
    pallas_call x1, Pallas kernels, shards(): pl.pallas_call(functools.partial(second_kernel, sizes), out_shape=[full,...  8.49 us
    pallas_call x1, Pallas kernels, shards(): pl.pallas_call(functools.partial(third_kernel, sizes), grid=(1,), out_sha...  6.71 us
    pallas_call x1, Pallas kernels, shards(): pl.pallas_call(functools.partial(first_kernel, sizes), out_shape=[full, *...  3.19 us
  transfers between devices with their start and end apart: 14, of which 4 were waited for; matrix products, arithmetic and copies ran while one was open for 1% of the time, Pallas kernels for 1%

commit v1 on v0

--- a/solution.py
+++ b/solution.py
@@ -33,14 +33,20 @@
     return jnp.where(ok, row, 0), ok
 
 
-def put_row(msg, row, ok, edge):
+ROWS = 5
+FIRST = pl.ds(0, 256, stride=ROWS)
+
+
+def put_row(msg, peer, ok, values, place=1):
+    row = ROWS * peer + place
     base = pl.ds(pl.multiple_of(row // 8 * 8, 8), 8)
     here = iota((8, 128), 0) == jnp.where(ok, row % 8, -1)
-    msg[base, 128:256] = jnp.where(here, edge, msg[base, 128:256])
-
-
-def take_row(got, row, ok, lanes):
-    rows = got[pl.ds(pl.multiple_of(row // 8 * 8, 8), 8), lanes]
+    msg[base, :] = jnp.where(here, values, msg[base, :])
+
+
+def take_row(got, peer, ok, place):
+    row = ROWS * peer + place
+    rows = got[pl.ds(pl.multiple_of(row // 8 * 8, 8), 8), :]
     here = iota((8, 128), 0) == jnp.where(ok, row % 8, -1)
     return jnp.sum(jnp.where(here, rows, 0.0), axis=0, keepdims=True)
 
@@ -94,7 +100,7 @@
     return jnp.where(alive, vstar, volt), calcium
 
 
-def send_faces(v, pos_ref, sizes, xlo, xhi, ylo, yhi, zlo, zhi, msg, lines):
+def send_faces(v, pos_ref, sizes, xlo, xhi, ylo, yhi, msg, lines):
     xlo[...] = v[0:2]
     xhi[...] = v[14:16]
     ylo[...] = v[:, 0:8, :]
@@ -103,8 +109,11 @@
     pick = ((row < 4) & (lane == jnp.where(row < 2, row, row + 124))).astype(F32)
     flat = v[...].reshape(CX * CY, CZ)
     ends = lax.dot_general(pick, flat, NT, precision=HIGHEST, preferred_element_type=F32)
-    zlo[...] = ends[0:2]
-    zhi[...] = ends[2:4]
+    for dz in (-1, 1):
+        peer, ok = neighbour(pos_ref, sizes, (0, 0, dz))
+        for n in range(4):
+            k, half = n // 2 + (2 if dz > 0 else 0), n % 2
+            put_row(msg, peer, ok, ends[k : k + 1, 128 * half : 128 * half + 128], 1 + n)
     lines[0:16] = v[0]
     lines[16:32] = v[15]
     for x in range(CX):
@@ -129,7 +138,7 @@
 
 def heads(pos_ref, sizes, got, step):
     row, ok = neighbour(pos_ref, sizes, step)
-    return take_row(got, row, ok, slice(0, 128))
+    return take_row(got, row, ok, 0)
 
 
 def entry(head, tile, which):
@@ -139,7 +148,7 @@
 
 def edges_of(pos_ref, sizes, got, step):
     row, ok = neighbour(pos_ref, sizes, step)
-    return take_row(got, row, ok, slice(128, 256))
+    return take_row(got, row, ok, 1)
 
 
 def tile_planes(pos_ref, sizes, got1, cx, cy, cz):
@@ -166,7 +175,7 @@
 
 
 def fill_extended(vext, v, faces, got, pos_ref, sizes):
-    xm, xp, ym, yp, zm, zp = faces
+    xm, xp, ym, yp = faces
     vext[2:18, 8:24, 0:128] = v[...]
     vext[0:2, 8:24, 0:128] = xm[...]
     vext[18:20, 8:24, 0:128] = xp[...]
@@ -174,7 +183,12 @@
     vext[2:18, 24:32, 0:128] = yp[...]
     row, lane = iota((8, 128), 0), iota((8, 128), 1)
     place = ((row < 4) & (lane == jnp.where(row < 2, row + 126, row - 2))).astype(F32)
-    outer = jnp.concatenate([zm[...], zp[...], jnp.zeros((4, 256), F32)], 0)
+    outer = []
+    for dz in (-1, 1):
+        peer, ok = neighbour(pos_ref, sizes, (0, 0, dz))
+        for k in range(2):
+            outer.append(jnp.concatenate([take_row(got, peer, ok, 1 + 2 * k + half) for half in range(2)], 1))
+    outer = jnp.concatenate([*outer, jnp.zeros((4, 256), F32)], 0)
     beyond = lax.dot_general(outer, place, TN, precision=HIGHEST, preferred_element_type=F32)
     vext[2:18, 8:24, 128:256] = beyond.reshape(16, 16, 128)
     for dx, i in ((-1, 1), (1, 18)):
@@ -228,6 +242,10 @@
     return 0.25 * (fx[x + 2] - fx[x] + dy + dz)
 
 
+def blocks(ref):
+    return jnp.concatenate([ref[n].T for n in range(8)], 0)
+
+
 def column_wide(values):
     return jnp.concatenate([jnp.broadcast_to(values[:, z : z + 1], (64, 256)) for z in range(4)], 0)
 
@@ -237,15 +255,15 @@
 
 
 def first_kernel(sizes, pos_ref, act_ref, fi_ref, half_ref, slope_ref, tau_ref, cond_ref, rev_ref, angle, conduct, block_elem,
-                 states, s1, xlo, xhi, ylo, yhi, zlo, zhi, msg, code_col, code_row, const, lines):
+                 states, s1, xlo, xhi, ylo, yhi, msg, code_col, code_row, const, lines):
     gate_constants(half_ref, slope_ref, tau_ref, cond_ref, rev_ref, const)
 
-    @pl.loop(0, CX)
+    @pl.loop(0, CX, unroll=2)
     def _(x):
-        alive = act_ref[x // 8, 0, 0] > 0
+        alive = act_ref[x // 8] > 0
         s1[0, x] = ionic_plane(states[0, x], states, s1, x, alive, const)[0]
 
-    ids = block_elem[...].reshape(64, 4)
+    ids = blocks(block_elem)
     owner = column_wide((ids // ELEMS).astype(F32))
     local = column_wide((ids % ELEMS).astype(F32))
     owner_row = to_row(owner)
@@ -265,8 +283,8 @@
     head = jnp.zeros((1, 128), F32)
     slots = iota((1, NF), 1)
     for tile in range(2):
-        alive = (act_ref[tile, 0, 0] > 0).astype(F32)
-        chosen = slots == fi_ref[tile, 0, 0]
+        alive = (act_ref[tile] > 0).astype(F32)
+        chosen = slots == fi_ref[tile]
         for n in range(6):
             value = jnp.sum(jnp.where(chosen, entries[n], 0.0), axis=1, keepdims=True) * alive
             head = jnp.where(lane == HEAD + 7 * tile + n, value, head)
@@ -277,9 +295,9 @@
         goes = (row_code == peers + 256.0 * r).astype(F32).astype(BF16)
         labels = jnp.where(target == r, local_row, 0.0).astype(BF16)
         asked += lax.dot_general(goes, labels, NT, preferred_element_type=F32)
-    msg[:, 0:128] = asked
-    msg[:, 128:256] = jnp.zeros((256, 128), F32)
-    send_faces(s1.at[0], pos_ref, sizes, xlo, xhi, ylo, yhi, zlo, zhi, msg, lines)
+    msg[...] = jnp.zeros((ROWS * 256, 128), F32)
+    msg[FIRST, :] = asked
+    send_faces(s1.at[0], pos_ref, sizes, xlo, xhi, ylo, yhi, msg, lines)
 
 
 def element_kernel(material, angle, node_disp, elem_node, elem_fibre, corner, passive, active):
@@ -330,17 +348,22 @@
     passive[...] = total[0:8] + total[8:16] + total[16:24]
 
 
-def second_kernel(sizes, pos_ref, half_ref, slope_ref, tau_ref, cond_ref, rev_ref, s1, xm, xp, ym, yp, zm, zp, got1, corner,
-                  code_row, block_weight, s2, xlo, xhi, ylo, yhi, zlo, zhi, msg, const, lines, vext, fx, cx, cy, cz, tens):
+def second_kernel(sizes, pos_ref, half_ref, slope_ref, tau_ref, cond_ref, rev_ref, s1, xm, xp, ym, yp, got1, corner,
+                  code_row, block_weight, s2, xlo, xhi, ylo, yhi, msg, const, lines, vext, fx, cx, cy, cz, tens):
     gate_constants(half_ref, slope_ref, tau_ref, cond_ref, rev_ref, const)
     live = tile_planes(pos_ref, sizes, got1, cx, cy, cz)
-    fill_extended(vext, s1.at[0], (xm, xp, ym, yp, zm, zp), got1, pos_ref, sizes)
+    fill_extended(vext, s1.at[0], (xm, xp, ym, yp), got1, pos_ref, sizes)
     flux_x(vext, fx, cx)
 
-    @pl.loop(0, CX)
+    @pl.loop(0, CX, unroll=4)
     def _(x):
         here = jnp.where(x < 8, live[0], live[1])
-        volt = s1[0, x] + here * lap_plane(vext, fx, cy, cz, x)
+        tens[x] = s1[0, x] + here * lap_plane(vext, fx, cy, cz, x)
+
+    @pl.loop(0, CX, unroll=2)
+    def _(x):
+        here = jnp.where(x < 8, live[0], live[1])
+        volt = tens[x]
         alive = jnp.broadcast_to(here, (16, 128)) > 0.5
         vstar, calcium = ionic_plane(volt, s1, s2, x, alive, const)
         s2[0, x] = vstar
@@ -353,41 +376,43 @@
     over_z = jnp.where(iota((128, 128), 0) // 32 == iota((128, 128), 1), 1.0 / 128.0, 0.0)
     mean = jnp.dot(over_y, pairs, precision=HIGHEST, preferred_element_type=F32)
     mean = jnp.dot(mean, over_z, precision=HIGHEST, preferred_element_type=F32)
-    value = to_row(column_wide(mean[:, 0:4] * block_weight[...].reshape(64, 4)))
+    value = to_row(column_wide(mean[:, 0:4] * blocks(block_weight)))
     peers = iota((256, 256), 0).astype(F32)
     elems = iota((256, 256), 1).astype(F32)
     target = iota((128, 256), 0)
     answer = jnp.zeros((256, 128), F32)
+    asked = got1[FIRST, :]
     none = jnp.zeros((64, 256), F32)
     for r in range(2):
         goes = (code_row[0:1, :] == peers + 256.0 * r).astype(F32).astype(BF16)
         for part in parts3(jnp.where(target == 64 * r + 3, value, 0.0)):
             answer += lax.dot_general(goes, part, NT, preferred_element_type=F32)
-        wants = (got1[:, r : r + 1] == elems + 1.0).astype(F32).astype(BF16)
+        wants = (asked[:, r : r + 1] == elems + 1.0).astype(F32).astype(BF16)
         held = jnp.concatenate([corner[...], none] if r == 0 else [none, corner[...]], 0)
         for part in parts3(held):
             answer += lax.dot_general(wants, part, NT, preferred_element_type=F32)
-    msg[:, 0:128] = answer
-    msg[:, 128:256] = jnp.zeros((256, 128), F32)
-    send_faces(s2.at[0], pos_ref, sizes, xlo, xhi, ylo, yhi, zlo, zhi, msg, lines)
-
-
-def third_kernel(sizes, pos_ref, s2, xm, xp, ym, yp, zm, zp, got1, got2, code_col, elem_node, passive, active, blend, s3, fine,
+    msg[...] = jnp.zeros((ROWS * 256, 128), F32)
+    msg[FIRST, :] = answer
+    send_faces(s2.at[0], pos_ref, sizes, xlo, xhi, ylo, yhi, msg, lines)
+
+
+def third_kernel(sizes, pos_ref, s2, xm, xp, ym, yp, got1, got2, code_col, elem_node, passive, active, blend, s3, fine,
                  residual, vext, fx, cx, cy, cz):
     live = tile_planes(pos_ref, sizes, got1, cx, cy, cz)
-    fill_extended(vext, s2.at[0], (xm, xp, ym, yp, zm, zp), got2, pos_ref, sizes)
+    fill_extended(vext, s2.at[0], (xm, xp, ym, yp), got2, pos_ref, sizes)
     flux_x(vext, fx, cx)
 
-    @pl.loop(0, CX)
+    @pl.loop(0, CX, unroll=4)
     def _(x):
         here = jnp.where(x < 8, live[0], live[1])
         s3[0, x] = s2[0, x] + here * lap_plane(vext, fx, cy, cz, x)
 
     elems = iota((256, 256), 1).astype(F32)
     tension = jnp.zeros((1, 256), F32)
+    asked, answer = got1[FIRST, :], got2[FIRST, :]
     for r in range(2):
-        wants = got1[:, r : r + 1] == elems + 1.0
-        tension += jnp.sum(jnp.where(wants, got2[:, 64 * r + 3 : 64 * r + 4], 0.0), axis=0, keepdims=True)
+        wants = asked[:, r : r + 1] == elems + 1.0
+        tension += jnp.sum(jnp.where(wants, answer[:, 64 * r + 3 : 64 * r + 4], 0.0), axis=0, keepdims=True)
     total = jnp.zeros((24, NODES), F32)
     for q in range(8):
         hot = (iota((NODES, ELEMS), 0) == elem_node[q : q + 1, :]).astype(F32).astype(BF16)
@@ -397,7 +422,6 @@
     residual[...] = total[0:3]
 
     code = jnp.concatenate([code_col[...], code_col[...]], 1)
-    answer = got2[:, 0:128]
     lane = iota((256, 128), 1)
     disp = jnp.zeros((256, 128), F32)
     for r in range(2):
@@ -449,27 +473,35 @@
     return lax.ppermute(x, axis, pairs)
 
 
-def exchange(xlo, xhi, ylo, yhi, zlo, zhi, msg):
-    got = lax.all_to_all(msg.reshape(256, 1, 256), ALL, 0, 0, tiled=True).reshape(256, 256)
-    return (
-        shift(xhi, "gx", 1),
-        shift(xlo, "gx", -1),
-        shift(yhi, "gy", 1),
-        shift(ylo, "gy", -1),
-        shift(zhi, "gz", 1),
-        shift(zlo, "gz", -1),
-    ), got
-
-
-SMEM = pl.BlockSpec(memory_space=pltpu.SMEM)
-VMEM = pl.BlockSpec(memory_space=pltpu.VMEM)
+def exchange(xlo, xhi, ylo, yhi, msg):
+    got = lax.all_to_all(msg.reshape(256, 1, ROWS * 128), ALL, 0, 0, tiled=True).reshape(ROWS * 256, 128)
+    halo = shift(xhi, "gx", 1), shift(xlo, "gx", -1), shift(yhi, "gy", 1), shift(ylo, "gy", -1)
+    return halo, got
+
+
+def whole(shape, space=None):
+    return pl.BlockSpec(shape, lambda i: (0,) * len(shape), memory_space=space)
+
+
+def call(body, name, scalars, arrays, outs, scratch=(), **more):
+    return pl.pallas_call(
+        body,
+        grid=(1,),
+        out_shape=outs,
+        in_specs=[whole(x.shape, pltpu.SMEM) for x in scalars] + [whole(x.shape) for x in arrays],
+        out_specs=[whole(x.shape) for x in outs],
+        scratch_shapes=scratch,
+        compiler_params=PARAMS,
+        name=name,
+        **more,
+    )(*scalars, *arrays)
 
 
 def sds(*shape):
     return jax.ShapeDtypeStruct(shape, F32)
 
 
-FACES = [sds(2, 16, 128), sds(2, 16, 128), sds(16, 8, 128), sds(16, 8, 128), sds(2, 256), sds(2, 256), sds(256, 256)]
+FACES = [sds(2, 16, 128), sds(2, 16, 128), sds(16, 8, 128), sds(16, 8, 128), sds(ROWS * 256, 128)]
 STEP_SCRATCH = [
     pltpu.VMEM((20, 32, 256), F32),
     pltpu.VMEM((18, 16, 128), F32),
@@ -478,7 +510,7 @@
     pltpu.VMEM((2, 3, 16, 256), F32),
 ]
 GATE_SCRATCH = [pltpu.VMEM((6 * NCH, 8, 128), F32), pltpu.VMEM((128, 128), F32)]
-PARAMS = pltpu.CompilerParams(vmem_limit_bytes=40 * 2**20)
+PARAMS = pltpu.CompilerParams(vmem_limit_bytes=60 * 2**20)
 
 
 def shards(states, active, fibre_index, fibre_angle, conduct, gate_half, gate_slope, gate_tau, conductance, reversal,
@@ -487,39 +519,32 @@
     pos = jnp.stack([lax.axis_index(a) for a in ALL]).astype(jnp.int32)
     gates = (gate_half, gate_slope, gate_tau, conductance, reversal)
     full = sds(NSTATE, CX, CY, CZ)
-    s1, *faces, code_col, code_row = pl.pallas_call(
+    s1, *faces, code_col, code_row = call(
         functools.partial(first_kernel, sizes),
-        out_shape=[full, *FACES, sds(256, 128), sds(8, 256)],
-        in_specs=[SMEM] * 8 + [VMEM] * 4,
-        out_specs=[VMEM] * 10,
-        scratch_shapes=GATE_SCRATCH,
-        compiler_params=PARAMS,
-        name="first",
-    )(pos, active, fibre_index, *gates, fibre_angle, conduct, block_elem, states)
+        "first",
+        (pos, active.reshape(2), fibre_index.reshape(2), *gates),
+        (fibre_angle, conduct, block_elem.transpose(0, 2, 1), states),
+        [full, *FACES, sds(256, 128), sds(8, 256)],
+        GATE_SCRATCH,
+    )
     halo, got1 = exchange(*faces)
-    corner, passive, active_force = pl.pallas_call(
+    corner, passive, active_force = call(
         element_kernel,
-        out_shape=[sds(64, ELEMS), sds(8, NODES), sds(64, ELEMS)],
-        in_specs=[SMEM] + [VMEM] * 4,
-        out_specs=[VMEM] * 3,
-        compiler_params=PARAMS,
-        name="elements",
-    )(material, fibre_angle, node_disp, elem_node, elem_fibre.reshape(1, ELEMS))
-    s2, *faces = pl.pallas_call(
+        "elements",
+        (material,),
+        (fibre_angle, node_disp, elem_node, elem_fibre.reshape(1, ELEMS)),
+        [sds(64, ELEMS), sds(8, NODES), sds(64, ELEMS)],
+    )
+    s2, *faces = call(
         functools.partial(second_kernel, sizes),
-        out_shape=[full, *FACES],
-        in_specs=[SMEM] * 6 + [VMEM] * 11,
-        out_specs=[VMEM] * 8,
-        scratch_shapes=GATE_SCRATCH + STEP_SCRATCH + [pltpu.VMEM((16, 16, 128), F32)],
-        compiler_params=PARAMS,
-        name="second",
-    )(pos, *gates, s1, *halo, got1, corner, code_row, block_weight)
+        "second",
+        (pos, *gates),
+        (s1, *halo, got1, corner, code_row, block_weight.transpose(0, 2, 1)),
+        [full, *FACES],
+        GATE_SCRATCH + STEP_SCRATCH + [pltpu.VMEM((16, 16, 128), F32)],
+    )
     halo, got2 = exchange(*faces)
-    plane = pl.BlockSpec((1, CX, CY, CZ), lambda i: (0, 0, 0, 0))
-
-    def whole(x):
-        return pl.BlockSpec(x.shape, lambda i: (0,) * x.ndim)
-
+    plane = whole((1, CX, CY, CZ))
     blend = jnp.asarray(blend_table())
     rest = (*halo, got1, got2, code_col, elem_node, passive, active_force, blend)
     outs = [full, sds(3, CX, CY, CZ), sds(3, NODES)]
@@ -527,8 +552,8 @@
         functools.partial(third_kernel, sizes),
         grid=(1,),
         out_shape=outs,
-        in_specs=[SMEM, plane, *[whole(x) for x in rest]],
-        out_specs=[plane, whole(outs[1]), whole(outs[2])],
+        in_specs=[whole((3,), pltpu.SMEM), plane, *[whole(x.shape) for x in rest]],
+        out_specs=[plane, whole(outs[1].shape), whole(outs[2].shape)],
         scratch_shapes=STEP_SCRATCH,
         input_output_aliases={1: 0},
         compiler_params=PARAMS,

time: 123 us -> 92 us (0.75)
  the two profiles are of different devices: /device:TPU:75 before, /device:TPU:1 now
where the time goes in v1:
time: 92 us; the launch traced here: 91.5 us
  starting transfers between devices  40.3 us (44%)
  waiting for transfers between devices  25.5 us (28%)
  Pallas kernels  22.6 us (25%)
  local copies, waits for them, and re-layouts  1.69 us (2%)
    all_to_all x2, starting transfers between devices, exchange(): lax.all_to_all(msg.reshape(256, 1, ROWS * 128), ALL, 0, 0, tiled=True)  21.9 us
    ppermute x8, starting transfers between devices, shift(): return lax.ppermute(x, axis, pairs)  18.4 us
    pallas_call x3, Pallas kernels, call(): pl.pallas_call(body, grid=(1,), out_shape=outs, in_specs=[whole(x.shape,...  17 us
    all_to_all x2, waiting for transfers between devices, exchange(): lax.all_to_all(msg.reshape(256, 1, ROWS * 128), ALL, 0, 0, tiled=True)  16 us
    ppermute x8, waiting for transfers between devices, shift(): return lax.ppermute(x, axis, pairs)  9.43 us
    pallas_call x1, Pallas kernels, shards(): pl.pallas_call(functools.partial(third_kernel, sizes), grid=(1,), out_sha...  5.63 us
  transfers between devices with their start and end apart: 10, of which 4 were waited for; matrix products, arithmetic and copies ran while one was open for 0% of the time, Pallas kernels for 3%

profile of v1, /device:TPU:1, one launch (start us, length us, event | category | flops | bytes accessed | tf_op | source)
XLA Modules:
  0.0 91.5 jit_solution(17095584494057282348)
XLA Ops:
  0.6 0.6 pad_add_fusion.pos_ref
  1.3 5.6 %first.1 = (f32[19,16,16,128]{3,2,1,0:T(8,128)}, f32[2,16,128]{2,1,0:T(8,128)}, f32[2,16,128]{2,1,0:T(8,128)}, f32[16,8,128]{2,1,0:T(8,128)}, f32[16,8,128]{2,1,...) custom-call(s32[3]{0:T(128)} %pad_add_fusion.pos_ref, s32[2]{0:T(128)} %bitcast.20, ...), custom_call_target="tpu_custom_call" | custom-call | tf_op jit(solution)/shard_map/first/pallas_call | solution.py:487
  6.9 15.7 %all-to-all-start = ((f32[256,1,640]{2,1,0:T(1,128)}), f32[256,1,640]{2,1,0:T(1,128)S(1)}, u32[]{:S(2)}, u32[]{:S(2)}) async-start(f32[256,1,640]{2,1,0:T(1,128)} %bitcast.16), calls=%async_computation | async-start | bytes 1310720 | tf_op jit(solution)/shard_map/all_to_all | solution.py:477
  22.5 3.3 %collective-permute-start.2 = (f32[16,8,128]{2,1,0:T(8,128)}, f32[16,8,128]{2,1,0:T(8,128)S(1)}, u32[]{:S(2)}, u32[]{:S(2)}) collective-permute-start(f32[16,8,128]{2,1,0:T(8,128)} %get-tuple-element.23), channel_id=1, source_target_pairs={{0,8},{8,16},{16,24},{1,9},{9,17},{17,25},{2,10},{10,18},{18,26},{... | collective-permute-start | bytes 196616 | tf_op jit(solution)/shard_map/ppermute | solution.py:473
  25.9 1.3 %collective-permute-start.3 = (f32[16,8,128]{2,1,0:T(8,128)}, f32[16,8,128]{2,1,0:T(8,128)S(1)}, u32[]{:S(2)}, u32[]{:S(2)}) collective-permute-start(f32[16,8,128]{2,1,0:T(8,128)} %get-tuple-element.24), channel_id=1, source_target_pairs={{8,0},{16,8},{24,16},{9,1},{17,9},{25,17},{10,2},{18,10},{26,18},{... | collective-permute-start | bytes 196616 | tf_op jit(solution)/shard_map/ppermute | solution.py:473
  27.2 3.3 %collective-permute-start = (f32[2,16,128]{2,1,0:T(8,128)}, f32[2,16,128]{2,1,0:T(8,128)S(1)}, u32[]{:S(2)}, u32[]{:S(2)}) collective-permute-start(f32[2,16,128]{2,1,0:T(8,128)} %get-tuple-element.21), channel_id=1, source_target_pairs={{0,32},{32,64},{64,96},{96,128},{128,160},{160,192},{192,224},{1,3... | collective-permute-start | bytes 49160 | tf_op jit(solution)/shard_map/ppermute | solution.py:473
  30.4 1.3 %collective-permute-start.1 = (f32[2,16,128]{2,1,0:T(8,128)}, f32[2,16,128]{2,1,0:T(8,128)S(1)}, u32[]{:S(2)}, u32[]{:S(2)}) collective-permute-start(f32[2,16,128]{2,1,0:T(8,128)} %get-tuple-element.22), channel_id=1, source_target_pairs={{32,0},{64,32},{96,64},{128,96},{160,128},{192,160},{224,192},{33,... | collective-permute-start | bytes 49160 | tf_op jit(solution)/shard_map/ppermute | solution.py:473
  31.7 2.7 %elements.1 = (f32[64,256]{1,0:T(8,128)}, f32[8,512]{1,0:T(8,128)}, f32[64,256]{1,0:T(8,128)}) custom-call(f32[3]{0:T(128)} %material.1, f32[2,64]{1,0:T(2,128)} %angle.3, f32[3,512]{1,0:T(4,128)} %node_disp.1, s32[8,256]{1,0:T(8,128)} %elem_node.3, s32[1,256]{1,0:T(1,128)} %bitcast.19), custom_call_target="tpu_custom_call" | custom-call | tf_op jit(solution)/shard_map/elements/pallas_call | solution.py:487
  34.4 0.0 collective-permute-done.xm
  34.4 3.4 %collective-permute-done.1.xp = f32[2,16,128]{2,1,0:T(8,128)S(1)} collective-permute-done((f32[2,16,128]{2,1,0:T(8,128)}, f32[2,16,128]{2,1,0:T(8,128)S(1)}, u32[]{:S(2)}, u32[]{:S(2)}) %collective-permute-start.1) | collective-permute-done | bytes 16416 | tf_op jit(solution)/shard_map/ppermute | solution.py:473
  37.8 0.0 copy-start.5
  37.8 8.0 %all-to-all-done = f32[256,1,640]{2,1,0:T(1,128)S(1)} async-done(((f32[256,1,640]{2,1,0:T(1,128)}), f32[256,1,640]{2,1,0:T(1,128)S(1)}, u32[]{:S(2)}, u32[]{:S(2)}) %all-to-all-start) | async-done | bytes 655392 | tf_op jit(solution)/shard_map/all_to_all | solution.py:477
  45.8 0.8 copy-done
  46.6 8.7 %second.1 = (f32[19,16,16,128]{3,2,1,0:T(8,128)}, f32[2,16,128]{2,1,0:T(8,128)}, f32[2,16,128]{2,1,0:T(8,128)}, f32[16,8,128]{2,1,0:T(8,128)}, f32[16,8,128]{2,1,0:T(8,128)}, /*index=5*/f32[1280,128]{1,0:T(8,128)}) custom-call(s32[3]{0:T(128)} %pad_add_fusion.pos_ref, f32[17]{0:T(128)} %half_ref.3, f32[17]{0:T(128)} %slope_ref.3, f32[17]{0:T(128)} %tau_ref.3, ...), custom_call_target="tpu_custom_call" | custom-call | tf_op jit(solution)/shard_map/second/pallas_call | solution.py:487
  55.4 6.2 %all-to-all-start.1 = ((f32[256,1,640]{2,1,0:T(1,128)}), f32[256,1,640]{2,1,0:T(1,128)S(1)}, u32[]{:S(2)}, u32[]{:S(2)}) async-start(f32[256,1,640]{2,1,0:T(1,128)} %bitcast.15), calls=%async_computation.1 | async-start | bytes 1310720 | tf_op jit(solution)/shard_map/all_to_all | solution.py:477
  61.6 3.4 %collective-permute-start.6 = (f32[16,8,128]{2,1,0:T(8,128)}, f32[16,8,128]{2,1,0:T(8,128)S(1)}, u32[]{:S(2)}, u32[]{:S(2)}) collective-permute-start(f32[16,8,128]{2,1,0:T(8,128)} %get-tuple-element.31), channel_id=1, source_target_pairs={{0,8},{8,16},{16,24},{1,9},{9,17},{17,25},{2,10},{10,18},{18,26},{... | collective-permute-start | bytes 196616 | tf_op jit(solution)/shard_map/ppermute | solution.py:473
  65.0 1.3 %collective-permute-start.7 = (f32[16,8,128]{2,1,0:T(8,128)}, f32[16,8,128]{2,1,0:T(8,128)S(1)}, u32[]{:S(2)}, u32[]{:S(2)}) collective-permute-start(f32[16,8,128]{2,1,0:T(8,128)} %get-tuple-element.32), channel_id=1, source_target_pairs={{8,0},{16,8},{24,16},{9,1},{17,9},{25,17},{10,2},{18,10},{26,18},{... | collective-permute-start | bytes 196616 | tf_op jit(solution)/shard_map/ppermute | solution.py:473
  66.3 3.4 %collective-permute-start.4 = (f32[2,16,128]{2,1,0:T(8,128)}, f32[2,16,128]{2,1,0:T(8,128)S(1)}, u32[]{:S(2)}, u32[]{:S(2)}) collective-permute-start(f32[2,16,128]{2,1,0:T(8,128)} %get-tuple-element.29), channel_id=1, source_target_pairs={{0,32},{32,64},{64,96},{96,128},{128,160},{160,192},{192,224},{1,3... | collective-permute-start | bytes 49160 | tf_op jit(solution)/shard_map/ppermute | solution.py:473
  69.6 1.3 %collective-permute-start.5 = (f32[2,16,128]{2,1,0:T(8,128)}, f32[2,16,128]{2,1,0:T(8,128)S(1)}, u32[]{:S(2)}, u32[]{:S(2)}) collective-permute-start(f32[2,16,128]{2,1,0:T(8,128)} %get-tuple-element.30), channel_id=1, source_target_pairs={{32,0},{64,32},{96,64},{128,96},{160,128},{192,160},{224,192},{33,... | collective-permute-start | bytes 49160 | tf_op jit(solution)/shard_map/ppermute | solution.py:473
  70.9 0.0 collective-permute-done.4.xm
  70.9 6.0 %collective-permute-done.5.xp = f32[2,16,128]{2,1,0:T(8,128)S(1)} collective-permute-done((f32[2,16,128]{2,1,0:T(8,128)}, f32[2,16,128]{2,1,0:T(8,128)S(1)}, u32[]{:S(2)}, u32[]{:S(2)}) %collective-permute-start.5) | collective-permute-done | bytes 16416 | tf_op jit(solution)/shard_map/ppermute | solution.py:473
  77.0 8.0 %all-to-all-done.1 = f32[256,1,640]{2,1,0:T(1,128)S(1)} async-done(((f32[256,1,640]{2,1,0:T(1,128)}), f32[256,1,640]{2,1,0:T(1,128)S(1)}, u32[]{:S(2)}, u32[]{:S(2)}) %all-to-all-start.1) | async-done | bytes 655392 | tf_op jit(solution)/shard_map/all_to_all | solution.py:477
  85.0 0.8 copy-done.1
  85.9 5.6 %third.1 = (f32[19,16,16,128]{3,2,1,0:T(8,128)}, f32[3,16,16,128]{3,2,1,0:T(8,128)}, f32[3,512]{1,0:T(4,128)}) custom-call(s32[3]{0:T(128)} %pad_add_fusion.pos_ref, f32[19,16,16,128]{3,2,1,0:T(8,128)} %get-tuple-element.28.s2, f32[2,16,128]{2,1,0:T(8,128)} %copy-done.6, f32[2,16,128]{2,1,0:T(8,128)} %copy-done.8, ...), custom_call_target="tpu_custom_call", output_to_operand_aliasing={{0}: (1, {})} | custom-call | tf_op jit(solution)/shard_map/third/pallas_call | solution.py:551
  (21 shorter events, 0.0 us)
Async XLA Ops:
  6.9 38.9 %all-to-all-start = ((f32[256,1,640]{2,1,0:T(1,128)}), f32[256,1,640]{2,1,0:T(1,128)S(1)}, u32[]{:S(2)}, u32[]{:S(2)}) async-start(f32[256,1,640]{2,1,0:T(1,128)} %bitcast.16), calls=%async_computation | async-start | bytes 1310720 | tf_op jit(solution)/shard_map/all_to_all | solution.py:477
  22.5 15.2 %collective-permute-start.2 = (f32[16,8,128]{2,1,0:T(8,128)}, f32[16,8,128]{2,1,0:T(8,128)S(1)}, u32[]{:S(2)}, u32[]{:S(2)}) collective-permute-start(f32[16,8,128]{2,1,0:T(8,128)} %get-tuple-element.23), channel_id=1, source_target_pairs={{0,8},{8,16},{16,24},{1,9},{9,17},{17,25},{2,10},{10,18},{18,26},{... | collective-permute-start | bytes 196616 | tf_op jit(solution)/shard_map/ppermute | solution.py:473
  25.9 11.9 %collective-permute-start.3 = (f32[16,8,128]{2,1,0:T(8,128)}, f32[16,8,128]{2,1,0:T(8,128)S(1)}, u32[]{:S(2)}, u32[]{:S(2)}) collective-permute-start(f32[16,8,128]{2,1,0:T(8,128)} %get-tuple-element.24), channel_id=1, source_target_pairs={{8,0},{16,8},{24,16},{9,1},{17,9},{25,17},{10,2},{18,10},{26,18},{... | collective-permute-start | bytes 196616 | tf_op jit(solution)/shard_map/ppermute | solution.py:473
  27.2 7.3 %collective-permute-start = (f32[2,16,128]{2,1,0:T(8,128)}, f32[2,16,128]{2,1,0:T(8,128)S(1)}, u32[]{:S(2)}, u32[]{:S(2)}) collective-permute-start(f32[2,16,128]{2,1,0:T(8,128)} %get-tuple-element.21), channel_id=1, source_target_pairs={{0,32},{32,64},{64,96},{96,128},{128,160},{160,192},{192,224},{1,3... | collective-permute-start | bytes 49160 | tf_op jit(solution)/shard_map/ppermute | solution.py:473
  30.4 7.3 %collective-permute-start.1 = (f32[2,16,128]{2,1,0:T(8,128)}, f32[2,16,128]{2,1,0:T(8,128)S(1)}, u32[]{:S(2)}, u32[]{:S(2)}) collective-permute-start(f32[2,16,128]{2,1,0:T(8,128)} %get-tuple-element.22), channel_id=1, source_target_pairs={{32,0},{64,32},{96,64},{128,96},{160,128},{192,160},{224,192},{33,... | collective-permute-start | bytes 49160 | tf_op jit(solution)/shard_map/ppermute | solution.py:473
  34.4 11.4 %copy-start.7 = (f32[2,16,128]{2,1,0:T(8,128)}, f32[2,16,128]{2,1,0:T(8,128)S(1)}, u32[]{:S(2)}) copy-start(f32[2,16,128]{2,1,0:T(8,128)S(1)} %collective-permute-done.xm) | copy-start | bytes 49156
  37.8 8.0 %copy-start.9 = (f32[2,16,128]{2,1,0:T(8,128)}, f32[2,16,128]{2,1,0:T(8,128)S(1)}, u32[]{:S(2)}) copy-start(f32[2,16,128]{2,1,0:T(8,128)S(1)} %collective-permute-done.1.xp) | copy-start | bytes 49156
  37.8 8.0 %copy-start.4 = (f32[16,8,128]{2,1,0:T(8,128)}, f32[16,8,128]{2,1,0:T(8,128)S(1)}, u32[]{:S(2)}) copy-start(f32[16,8,128]{2,1,0:T(8,128)S(1)} %collective-permute-done.2.ym) | copy-start | bytes 196612
  37.8 8.0 %copy-start.5 = (f32[16,8,128]{2,1,0:T(8,128)}, f32[16,8,128]{2,1,0:T(8,128)S(1)}, u32[]{:S(2)}) copy-start(f32[16,8,128]{2,1,0:T(8,128)S(1)} %collective-permute-done.3.yp) | copy-start | bytes 196612
  45.8 0.8 copy-start
  55.4 29.6 %all-to-all-start.1 = ((f32[256,1,640]{2,1,0:T(1,128)}), f32[256,1,640]{2,1,0:T(1,128)S(1)}, u32[]{:S(2)}, u32[]{:S(2)}) async-start(f32[256,1,640]{2,1,0:T(1,128)} %bitcast.15), calls=%async_computation.1 | async-start | bytes 1310720 | tf_op jit(solution)/shard_map/all_to_all | solution.py:477
  61.6 15.4 %collective-permute-start.6 = (f32[16,8,128]{2,1,0:T(8,128)}, f32[16,8,128]{2,1,0:T(8,128)S(1)}, u32[]{:S(2)}, u32[]{:S(2)}) collective-permute-start(f32[16,8,128]{2,1,0:T(8,128)} %get-tuple-element.31), channel_id=1, source_target_pairs={{0,8},{8,16},{16,24},{1,9},{9,17},{17,25},{2,10},{10,18},{18,26},{... | collective-permute-start | bytes 196616 | tf_op jit(solution)/shard_map/ppermute | solution.py:473
  65.0 12.0 %collective-permute-start.7 = (f32[16,8,128]{2,1,0:T(8,128)}, f32[16,8,128]{2,1,0:T(8,128)S(1)}, u32[]{:S(2)}, u32[]{:S(2)}) collective-permute-start(f32[16,8,128]{2,1,0:T(8,128)} %get-tuple-element.32), channel_id=1, source_target_pairs={{8,0},{16,8},{24,16},{9,1},{17,9},{25,17},{10,2},{18,10},{26,18},{... | collective-permute-start | bytes 196616 | tf_op jit(solution)/shard_map/ppermute | solution.py:473
  66.3 4.7 %collective-permute-start.4 = (f32[2,16,128]{2,1,0:T(8,128)}, f32[2,16,128]{2,1,0:T(8,128)S(1)}, u32[]{:S(2)}, u32[]{:S(2)}) collective-permute-start(f32[2,16,128]{2,1,0:T(8,128)} %get-tuple-element.29), channel_id=1, source_target_pairs={{0,32},{32,64},{64,96},{96,128},{128,160},{160,192},{192,224},{1,3... | collective-permute-start | bytes 49160 | tf_op jit(solution)/shard_map/ppermute | solution.py:473
  69.6 7.3 %collective-permute-start.5 = (f32[2,16,128]{2,1,0:T(8,128)}, f32[2,16,128]{2,1,0:T(8,128)S(1)}, u32[]{:S(2)}, u32[]{:S(2)}) collective-permute-start(f32[2,16,128]{2,1,0:T(8,128)} %get-tuple-element.30), channel_id=1, source_target_pairs={{32,0},{64,32},{96,64},{128,96},{160,128},{192,160},{224,192},{33,... | collective-permute-start | bytes 49160 | tf_op jit(solution)/shard_map/ppermute | solution.py:473
  70.9 14.1 %copy-start.6 = (f32[2,16,128]{2,1,0:T(8,128)}, f32[2,16,128]{2,1,0:T(8,128)S(1)}, u32[]{:S(2)}) copy-start(f32[2,16,128]{2,1,0:T(8,128)S(1)} %collective-permute-done.4.xm) | copy-start | bytes 49156
  77.0 8.1 %copy-start.8 = (f32[2,16,128]{2,1,0:T(8,128)}, f32[2,16,128]{2,1,0:T(8,128)S(1)}, u32[]{:S(2)}) copy-start(f32[2,16,128]{2,1,0:T(8,128)S(1)} %collective-permute-done.5.xp) | copy-start | bytes 49156
  77.0 8.1 %copy-start.2 = (f32[16,8,128]{2,1,0:T(8,128)}, f32[16,8,128]{2,1,0:T(8,128)S(1)}, u32[]{:S(2)}) copy-start(f32[16,8,128]{2,1,0:T(8,128)S(1)} %collective-permute-done.6.ym) | copy-start | bytes 196612
  77.0 8.1 %copy-start.3 = (f32[16,8,128]{2,1,0:T(8,128)}, f32[16,8,128]{2,1,0:T(8,128)S(1)}, u32[]{:S(2)}) copy-start(f32[16,8,128]{2,1,0:T(8,128)S(1)} %collective-permute-done.7.yp) | copy-start | bytes 196612
  85.0 0.9 copy-start.1

commit v2 on v1

--- a/solution.py
+++ b/solution.py
@@ -41,11 +41,11 @@
     row = ROWS * peer + place
     base = pl.ds(pl.multiple_of(row // 8 * 8, 8), 8)
     here = iota((8, 128), 0) == jnp.where(ok, row % 8, -1)
-    msg[base, :] = jnp.where(here, values, msg[base, :])
-
-
-def take_row(got, peer, ok, place):
-    row = ROWS * peer + place
+    pltpu.store(msg.at[base, :], jnp.broadcast_to(values, (8, 128)), mask=here)
+
+
+def take_row(got, peer, ok, place, rows_each=ROWS):
+    row = rows_each * peer + place
     rows = got[pl.ds(pl.multiple_of(row // 8 * 8, 8), 8), :]
     here = iota((8, 128), 0) == jnp.where(ok, row % 8, -1)
     return jnp.sum(jnp.where(here, rows, 0.0), axis=0, keepdims=True)
@@ -77,27 +77,61 @@
         const[5 * NCH + c] = cond * rev_ref[c]
 
 
+GROUPS = ((0, 1), (1, 5), (5, 9), (9, 13), (13, 17), (17, NSTATE))
+
+
+def fetches(hbm, vmem, sems):
+    copies = []
+    for n, (low, high) in enumerate(GROUPS):
+        copies.append(pltpu.make_async_copy(hbm.at[low:high], vmem.at[low:high], sems.at[n]))
+        copies[n].start()
+    return copies
+
+
+def drain(vmem, hbm, sems, n):
+    low, high = GROUPS[n]
+    copy = pltpu.make_async_copy(vmem.at[low:high], hbm.at[low:high], sems.at[n])
+    copy.start()
+    return copy
+
+
 def twice(x):
     return jnp.concatenate([x, x], 0)
 
 
-def ionic_plane(volt, source, target, x, alive, const):
-    total = jnp.zeros_like(volt)
-    moment = jnp.zeros_like(volt)
-    for c in range(NCH):
-        rise = jnp.tanh(volt * twice(const[c]) + twice(const[NCH + c]))
-        old = source[1 + c, x]
-        lift = twice(const[3 * NCH + c])
-        gate = old * twice(const[2 * NCH + c]) + (lift * rise + lift)
-        total += gate * twice(const[4 * NCH + c])
-        moment += gate * twice(const[5 * NCH + c])
-        target[1 + c, x] = jnp.where(alive, gate, old)
-    vstar = volt - (volt * total - moment)
-    old = source[NSTATE - 1, x]
-    calcium = old * 0.9 + 0.1 * (0.5 * jnp.tanh(4.0 * (volt - 0.5)) + 0.5)
-    calcium = jnp.where(alive, calcium, old)
-    target[NSTATE - 1, x] = calcium
-    return jnp.where(alive, vstar, volt), calcium
+def ionic_step(volt, source, target, alive, const, total, moment, coming, hbm, left):
+    leaving = []
+    for n, (low, high) in enumerate(GROUPS):
+        if coming[n] is not None:
+            coming[n].wait()
+        for s in range(max(low, 1), high):
+            c = s - 1
+            for half in range(2):
+
+                @pl.loop(8 * half, 8 * half + 8, unroll=8)
+                def _(x):
+                    old = source[s, x]
+                    if s < NSTATE - 1:
+                        rise = jnp.tanh(volt[x] * twice(const[c]) + twice(const[NCH + c]))
+                        lift = twice(const[3 * NCH + c])
+                        new = old * twice(const[2 * NCH + c]) + (lift * rise + lift)
+                        flow, shift_ = new * twice(const[4 * NCH + c]), new * twice(const[5 * NCH + c])
+                        total[x] = flow if c == 0 else total[x] + flow
+                        moment[x] = shift_ if c == 0 else moment[x] + shift_
+                    else:
+                        new = old * 0.9 + 0.1 * (0.5 * jnp.tanh(4.0 * (volt[x] - 0.5)) + 0.5)
+                    target[s, x] = jnp.where(alive[half], new, old)
+
+        if n:
+            leaving.append(drain(target, hbm, left, n))
+    for half in range(2):
+
+        @pl.loop(8 * half, 8 * half + 8, unroll=8)
+        def _(x):
+            v = volt[x]
+            target[0, x] = jnp.where(alive[half], v - (v * total[x] - moment[x]), v)
+
+    return [*leaving, drain(target, hbm, left, 0)]
 
 
 def send_faces(v, pos_ref, sizes, xlo, xhi, ylo, yhi, msg, lines):
@@ -138,7 +172,7 @@
 
 def heads(pos_ref, sizes, got, step):
     row, ok = neighbour(pos_ref, sizes, step)
-    return take_row(got, row, ok, 0)
+    return take_row(got, row, ok, 0, 1)
 
 
 def entry(head, tile, which):
@@ -255,14 +289,9 @@
 
 
 def first_kernel(sizes, pos_ref, act_ref, fi_ref, half_ref, slope_ref, tau_ref, cond_ref, rev_ref, angle, conduct, block_elem,
-                 states, s1, xlo, xhi, ylo, yhi, msg, code_col, code_row, const, lines):
+                 states_hbm, s1_hbm, xlo, xhi, ylo, yhi, msg, code_col, code_row, const, lines, states, s1, came, left, total, moment):
+    coming = fetches(states_hbm, states, came)
     gate_constants(half_ref, slope_ref, tau_ref, cond_ref, rev_ref, const)
-
-    @pl.loop(0, CX, unroll=2)
-    def _(x):
-        alive = act_ref[x // 8] > 0
-        s1[0, x] = ionic_plane(states[0, x], states, s1, x, alive, const)[0]
-
     ids = blocks(block_elem)
     owner = column_wide((ids // ELEMS).astype(F32))
     local = column_wide((ids % ELEMS).astype(F32))
@@ -297,7 +326,11 @@
         asked += lax.dot_general(goes, labels, NT, preferred_element_type=F32)
     msg[...] = jnp.zeros((ROWS * 256, 128), F32)
     msg[FIRST, :] = asked
+    alive = [act_ref[half] > 0 for half in range(2)]
+    leaving = ionic_step(states.at[0], states, s1, alive, const, total, moment, coming, s1_hbm, left)
     send_faces(s1.at[0], pos_ref, sizes, xlo, xhi, ylo, yhi, msg, lines)
+    for copy in leaving:
+        copy.wait()
 
 
 def element_kernel(material, angle, node_disp, elem_node, elem_fibre, corner, passive, active):
@@ -348,10 +381,14 @@
     passive[...] = total[0:8] + total[8:16] + total[16:24]
 
 
-def second_kernel(sizes, pos_ref, half_ref, slope_ref, tau_ref, cond_ref, rev_ref, s1, xm, xp, ym, yp, got1, corner,
-                  code_row, block_weight, s2, xlo, xhi, ylo, yhi, msg, const, lines, vext, fx, cx, cy, cz, tens):
+def second_kernel(sizes, pos_ref, half_ref, slope_ref, tau_ref, cond_ref, rev_ref, s1_hbm, xm, xp, ym, yp, got1, corner,
+                  code_row, block_weight, s2_hbm, xlo, xhi, ylo, yhi, msg, heard, const, lines, s1, s2, came, left, total, moment, vext, fx, cx, cy, cz,
+                  tens):
+    coming = fetches(s1_hbm, s1, came)
     gate_constants(half_ref, slope_ref, tau_ref, cond_ref, rev_ref, const)
-    live = tile_planes(pos_ref, sizes, got1, cx, cy, cz)
+    heard[...] = got1[FIRST, :]
+    live = tile_planes(pos_ref, sizes, heard, cx, cy, cz)
+    coming[0].wait()
     fill_extended(vext, s1.at[0], (xm, xp, ym, yp), got1, pos_ref, sizes)
     flux_x(vext, fx, cx)
 
@@ -360,17 +397,15 @@
         here = jnp.where(x < 8, live[0], live[1])
         tens[x] = s1[0, x] + here * lap_plane(vext, fx, cy, cz, x)
 
-    @pl.loop(0, CX, unroll=2)
-    def _(x):
-        here = jnp.where(x < 8, live[0], live[1])
-        volt = tens[x]
-        alive = jnp.broadcast_to(here, (16, 128)) > 0.5
-        vstar, calcium = ionic_plane(volt, s1, s2, x, alive, const)
-        s2[0, x] = vstar
-        square = calcium * calcium
-        tens[x] = square / (square + 0.09)
-
-    pairs = jnp.concatenate([tens[2 * n] + tens[2 * n + 1] for n in range(8)], 0)
+    alive = [jnp.broadcast_to(here, (16, 128)) > 0.5 for here in live]
+    leaving = ionic_step(tens, s1, s2, alive, const, total, moment, [None, *coming[1:]], s2_hbm, left)
+    for n in range(8):
+        ratio = jnp.zeros((16, 128), F32)
+        for x in (2 * n, 2 * n + 1):
+            square = s2[NSTATE - 1, x] * s2[NSTATE - 1, x]
+            ratio += square / (square + 0.09)
+        lines[16 * n : 16 * n + 16] = ratio
+    pairs = lines[...]
     row, lane = iota((64, 128), 0), iota((64, 128), 1)
     over_y = ((row // 8 == lane // 16) & (row % 8 == lane % 16 // 2)).astype(F32)
     over_z = jnp.where(iota((128, 128), 0) // 32 == iota((128, 128), 1), 1.0 / 128.0, 0.0)
@@ -381,7 +416,7 @@
     elems = iota((256, 256), 1).astype(F32)
     target = iota((128, 256), 0)
     answer = jnp.zeros((256, 128), F32)
-    asked = got1[FIRST, :]
+    asked = heard[...]
     none = jnp.zeros((64, 256), F32)
     for r in range(2):
         goes = (code_row[0:1, :] == peers + 256.0 * r).astype(F32).astype(BF16)
@@ -389,16 +424,20 @@
             answer += lax.dot_general(goes, part, NT, preferred_element_type=F32)
         wants = (asked[:, r : r + 1] == elems + 1.0).astype(F32).astype(BF16)
         held = jnp.concatenate([corner[...], none] if r == 0 else [none, corner[...]], 0)
-        for part in parts3(held):
+        for part in parts3(held)[:2]:
             answer += lax.dot_general(wants, part, NT, preferred_element_type=F32)
     msg[...] = jnp.zeros((ROWS * 256, 128), F32)
     msg[FIRST, :] = answer
     send_faces(s2.at[0], pos_ref, sizes, xlo, xhi, ylo, yhi, msg, lines)
-
-
-def third_kernel(sizes, pos_ref, s2, xm, xp, ym, yp, got1, got2, code_col, elem_node, passive, active, blend, s3, fine,
-                 residual, vext, fx, cx, cy, cz):
-    live = tile_planes(pos_ref, sizes, got1, cx, cy, cz)
+    for copy in leaving:
+        copy.wait()
+
+
+def third_kernel(sizes, pos_ref, s2, xm, xp, ym, yp, heard, got2, code_col, elem_node, passive, active, blend_hbm, s3, fine,
+                 residual, vext, fx, cx, cy, cz, blend, came):
+    coming = pltpu.make_async_copy(blend_hbm, blend, came)
+    coming.start()
+    live = tile_planes(pos_ref, sizes, heard, cx, cy, cz)
     fill_extended(vext, s2.at[0], (xm, xp, ym, yp), got2, pos_ref, sizes)
     flux_x(vext, fx, cx)
 
@@ -409,7 +448,7 @@
 
     elems = iota((256, 256), 1).astype(F32)
     tension = jnp.zeros((1, 256), F32)
-    asked, answer = got1[FIRST, :], got2[FIRST, :]
+    asked, answer = heard[...], got2[FIRST, :]
     for r in range(2):
         wants = asked[:, r : r + 1] == elems + 1.0
         tension += jnp.sum(jnp.where(wants, answer[:, 64 * r + 3 : 64 * r + 4], 0.0), axis=0, keepdims=True)
@@ -428,14 +467,15 @@
         goes = (code == elems + 256.0 * r).astype(F32).astype(BF16)
         part = jnp.where(lane // 64 == r, answer, 0.0)
         part = part if r == 0 else pltpu.roll(part, 64, 1)
-        for piece in parts3(part):
+        for piece in parts3(part)[:2]:
             disp += jnp.dot(goes, piece, preferred_element_type=F32)
     merged = jnp.concatenate(
         [disp[0:64] + pltpu.roll(disp[64:128], 64, 1), disp[128:192] + pltpu.roll(disp[192:256], 64, 1)], 1
     )
     which = iota((64, 256), 1) % 8
     rows = jnp.concatenate([jnp.where(which == c, merged, 0.0) for c in range(3)], 0)
-    first, second, third = parts3(rows)
+    first, second, _ = parts3(rows)
+    coming.wait()
     out = jnp.dot(first, blend[0], preferred_element_type=F32) + jnp.dot(second, blend[0], preferred_element_type=F32)
     out += jnp.dot(first, blend[1], preferred_element_type=F32)
     for c in range(3):
@@ -483,17 +523,20 @@
     return pl.BlockSpec(shape, lambda i: (0,) * len(shape), memory_space=space)
 
 
-def call(body, name, scalars, arrays, outs, scratch=(), **more):
+ANYWHERE = pl.BlockSpec(memory_space=pl.ANY)
+
+
+def call(body, name, scalars, arrays, outs, scratch=(), far=(), mebibytes=50):
+    specs = [ANYWHERE if n in far else whole(x.shape) for n, x in enumerate([*arrays, *outs])]
     return pl.pallas_call(
         body,
         grid=(1,),
         out_shape=outs,
-        in_specs=[whole(x.shape, pltpu.SMEM) for x in scalars] + [whole(x.shape) for x in arrays],
-        out_specs=[whole(x.shape) for x in outs],
+        in_specs=[whole(x.shape, pltpu.SMEM) for x in scalars] + specs[: len(arrays)],
+        out_specs=specs[len(arrays) :],
         scratch_shapes=scratch,
-        compiler_params=PARAMS,
+        compiler_params=grant(mebibytes),
         name=name,
-        **more,
     )(*scalars, *arrays)
 
 
@@ -509,8 +552,17 @@
     pltpu.VMEM((2, 3, 32, 128), F32),
     pltpu.VMEM((2, 3, 16, 256), F32),
 ]
+STATE_SCRATCH = [
+    pltpu.VMEM((NSTATE, CX, CY, CZ), F32),
+    pltpu.VMEM((NSTATE, CX, CY, CZ), F32),
+    pltpu.SemaphoreType.DMA((len(GROUPS),)),
+    pltpu.SemaphoreType.DMA((len(GROUPS),)),
+    pltpu.VMEM((CX, CY, CZ), F32),
+    pltpu.VMEM((CX, CY, CZ), F32),
+]
 GATE_SCRATCH = [pltpu.VMEM((6 * NCH, 8, 128), F32), pltpu.VMEM((128, 128), F32)]
-PARAMS = pltpu.CompilerParams(vmem_limit_bytes=60 * 2**20)
+def grant(mebibytes):
+    return pltpu.CompilerParams(vmem_limit_bytes=mebibytes * 2**20)
 
 
 def shards(states, active, fibre_index, fibre_angle, conduct, gate_half, gate_slope, gate_tau, conductance, reversal,
@@ -525,7 +577,9 @@
         (pos, active.reshape(2), fibre_index.reshape(2), *gates),
         (fibre_angle, conduct, block_elem.transpose(0, 2, 1), states),
         [full, *FACES, sds(256, 128), sds(8, 256)],
-        GATE_SCRATCH,
+        GATE_SCRATCH + STATE_SCRATCH,
+        (3, 4),
+        60,
     )
     halo, got1 = exchange(*faces)
     corner, passive, active_force = call(
@@ -535,30 +589,31 @@
         (fibre_angle, node_disp, elem_node, elem_fibre.reshape(1, ELEMS)),
         [sds(64, ELEMS), sds(8, NODES), sds(64, ELEMS)],
     )
-    s2, *faces = call(
+    s2, *faces, heard = call(
         functools.partial(second_kernel, sizes),
         "second",
         (pos, *gates),
         (s1, *halo, got1, corner, code_row, block_weight.transpose(0, 2, 1)),
-        [full, *FACES],
-        GATE_SCRATCH + STEP_SCRATCH + [pltpu.VMEM((16, 16, 128), F32)],
+        [full, *FACES, sds(256, 128)],
+        GATE_SCRATCH + STATE_SCRATCH + STEP_SCRATCH + [pltpu.VMEM((16, 16, 128), F32)],
+        (0, 9),
     )
     halo, got2 = exchange(*faces)
     plane = whole((1, CX, CY, CZ))
     blend = jnp.asarray(blend_table())
-    rest = (*halo, got1, got2, code_col, elem_node, passive, active_force, blend)
+    rest = (*halo, heard, got2, code_col, elem_node, passive, active_force)
     outs = [full, sds(3, CX, CY, CZ), sds(3, NODES)]
     return pl.pallas_call(
         functools.partial(third_kernel, sizes),
         grid=(1,),
         out_shape=outs,
-        in_specs=[whole((3,), pltpu.SMEM), plane, *[whole(x.shape) for x in rest]],
+        in_specs=[whole((3,), pltpu.SMEM), plane, *[whole(x.shape) for x in rest], ANYWHERE],
         out_specs=[plane, whole(outs[1].shape), whole(outs[2].shape)],
-        scratch_shapes=STEP_SCRATCH,
+        scratch_shapes=STEP_SCRATCH + [pltpu.VMEM(blend.shape, BF16), pltpu.SemaphoreType.DMA],
         input_output_aliases={1: 0},
-        compiler_params=PARAMS,
+        compiler_params=grant(50),
         name="third",
-    )(pos, s2, *rest)
+    )(pos, s2, *rest, blend)
 
 
 def solution(mesh):

time: 92 us -> 89.2 us (0.970)
  Pallas kernels: 22.6 us -> 19.7 us
    pallas_call x3, Pallas kernels: 17 us -> 14.5 us  [call(): pl.pallas_call(body, grid=(1,), out_shape=outs, in_specs=[whole(x.shape,...]
    unnamed x20 -> x30, local copies, waits for them, and re-layouts: 1.69 us -> 0.77 us
  transfers between devices with their start and end apart: 10 -> 10, of which waited for: 4 -> 4; matrix products, arithmetic and copies ran while one was open for 0% -> 0% of each run, Pallas kernels for 3% -> 2%
where the time goes in v2:
time: 89.2 us; the launch traced here: 88.6 us
  starting transfers between devices  40.5 us (45%)
  waiting for transfers between devices  26.2 us (29%)
  Pallas kernels  19.7 us (22%)
  between operations  0.94 us (1%)
    all_to_all x2, starting transfers between devices, exchange(): lax.all_to_all(msg.reshape(256, 1, ROWS * 128), ALL, 0, 0, tiled=True)  22 us
    ppermute x8, starting transfers between devices, shift(): return lax.ppermute(x, axis, pairs)  18.5 us
    all_to_all x2, waiting for transfers between devices, exchange(): lax.all_to_all(msg.reshape(256, 1, ROWS * 128), ALL, 0, 0, tiled=True)  16.1 us
    pallas_call x3, Pallas kernels, call(): pl.pallas_call(body, grid=(1,), out_shape=outs, in_specs=[whole(x.shape,...  14.5 us
    ppermute x8, waiting for transfers between devices, shift(): return lax.ppermute(x, axis, pairs)  10.1 us
    pallas_call x1, Pallas kernels, shards(): pl.pallas_call(functools.partial(third_kernel, sizes), grid=(1,), out_sha...  5.25 us
  transfers between devices with their start and end apart: 10, of which 4 were waited for; matrix products, arithmetic and copies ran while one was open for 0% of the time, Pallas kernels for 2%

profile of v2, /device:TPU:1, one launch (start us, length us, event | category | flops | bytes accessed | tf_op | source)
XLA Modules:
  0.0 88.6 jit_solution(9555505250699528294)
XLA Ops:
  0.6 0.0 copy-start.11
  0.7 0.0 copy-start.10
  0.8 0.6 pad_add_fusion.pos_ref
  1.3 5.5 %first.1 = (f32[19,16,16,128]{3,2,1,0:T(8,128)}, f32[2,16,128]{2,1,0:T(8,128)}, f32[2,16,128]{2,1,0:T(8,128)}, f32[16,8,128]{2,1,0:T(8,128)}, f32[16,8,128]{2,1,...) custom-call(s32[3]{0:T(128)} %pad_add_fusion.pos_ref, s32[2]{0:T(128)} %bitcast.18, ...), custom_call_target="tpu_custom_call" | custom-call | tf_op jit(solution)/shard_map/first/pallas_call | solution.py:531
  6.8 15.7 %all-to-all-start = ((f32[256,1,640]{2,1,0:T(1,128)}), f32[256,1,640]{2,1,0:T(1,128)S(1)}, u32[]{:S(2)}, u32[]{:S(2)}) async-start(f32[256,1,640]{2,1,0:T(1,128)} %bitcast.16), calls=%async_computation | async-start | bytes 1310720 | tf_op jit(solution)/shard_map/all_to_all | solution.py:517
  22.5 0.0 copy-start
  22.5 3.4 %collective-permute-start.2 = (f32[16,8,128]{2,1,0:T(8,128)}, f32[16,8,128]{2,1,0:T(8,128)S(1)}, u32[]{:S(2)}, u32[]{:S(2)}) collective-permute-start(f32[16,8,128]{2,1,0:T(8,128)} %get-tuple-element.24), channel_id=1, source_target_pairs={{0,8},{8,16},{16,24},{1,9},{9,17},{17,25},{2,10},{10,18},{18,26},{... | collective-permute-start | bytes 196616 | tf_op jit(solution)/shard_map/ppermute | solution.py:513
  26.0 1.3 %collective-permute-start.3 = (f32[16,8,128]{2,1,0:T(8,128)}, f32[16,8,128]{2,1,0:T(8,128)S(1)}, u32[]{:S(2)}, u32[]{:S(2)}) collective-permute-start(f32[16,8,128]{2,1,0:T(8,128)} %get-tuple-element.25), channel_id=1, source_target_pairs={{8,0},{16,8},{24,16},{9,1},{17,9},{25,17},{10,2},{18,10},{26,18},{... | collective-permute-start | bytes 196616 | tf_op jit(solution)/shard_map/ppermute | solution.py:513
  27.3 3.3 %collective-permute-start = (f32[2,16,128]{2,1,0:T(8,128)}, f32[2,16,128]{2,1,0:T(8,128)S(1)}, u32[]{:S(2)}, u32[]{:S(2)}) collective-permute-start(f32[2,16,128]{2,1,0:T(8,128)} %get-tuple-element.22), channel_id=1, source_target_pairs={{0,32},{32,64},{64,96},{96,128},{128,160},{160,192},{192,224},{1,3... | collective-permute-start | bytes 49160 | tf_op jit(solution)/shard_map/ppermute | solution.py:513
  30.6 1.3 %collective-permute-start.1 = (f32[2,16,128]{2,1,0:T(8,128)}, f32[2,16,128]{2,1,0:T(8,128)S(1)}, u32[]{:S(2)}, u32[]{:S(2)}) collective-permute-start(f32[2,16,128]{2,1,0:T(8,128)} %get-tuple-element.23), channel_id=1, source_target_pairs={{32,0},{64,32},{96,64},{128,96},{160,128},{192,160},{224,192},{33,... | collective-permute-start | bytes 49160 | tf_op jit(solution)/shard_map/ppermute | solution.py:513
  31.9 1.8 %elements.1 = (f32[64,256]{1,0:T(8,128)S(1)}, f32[8,512]{1,0:T(8,128)S(1)}, f32[64,256]{1,0:T(8,128)S(1)}) custom-call(f32[3]{0:T(128)S(1)} %copy-done.14, f32[2,64]{1,0:T(2,128)S(1)} %copy-done.7, f32[3,512]{1,0:T(4,128)S(1)} %copy-done.5, s32[8,256]{1,0:T(8,128)S(1)} %copy-done.2, s32[1,256]{1,0:T(1,128)S(1)} %bitcast.15), custom_call_target="tpu_custom_call" | custom-call | tf_op jit(solution)/shard_map/elements/pallas_call | solution.py:531
  33.7 0.0 collective-permute-done.xm
  33.7 4.1 %collective-permute-done.1.xp = f32[2,16,128]{2,1,0:T(8,128)S(1)} collective-permute-done((f32[2,16,128]{2,1,0:T(8,128)}, f32[2,16,128]{2,1,0:T(8,128)S(1)}, u32[]{:S(2)}, u32[]{:S(2)}) %collective-permute-start.1) | collective-permute-done | bytes 16416 | tf_op jit(solution)/shard_map/ppermute | solution.py:513
  37.8 8.0 %all-to-all-done = f32[256,1,640]{2,1,0:T(1,128)S(1)} async-done(((f32[256,1,640]{2,1,0:T(1,128)}), f32[256,1,640]{2,1,0:T(1,128)S(1)}, u32[]{:S(2)}, u32[]{:S(2)}) %all-to-all-start) | async-done | bytes 655392 | tf_op jit(solution)/shard_map/all_to_all | solution.py:517
  45.8 0.7 copy-done.4
  46.5 7.2 %second.1 = (f32[19,16,16,128]{3,2,1,0:T(8,128)}, f32[2,16,128]{2,1,0:T(8,128)S(1)}, f32[2,16,128]{2,1,0:T(8,128)S(1)}, f32[16,8,128]{2,1,0:T(8,128)S(1)}, f32[1...) custom-call(s32[3]{0:T(128)S(1)} %copy-done.6, f32[17]{0:T(128)S(1)} %copy-done.8, ...), custom_call_target="tpu_custom_call" | custom-call | tf_op jit(solution)/shard_map/second/pallas_call | solution.py:531
  53.7 6.3 %all-to-all-start.1 = ((f32[256,1,640]{2,1,0:T(1,128)}), f32[256,1,640]{2,1,0:T(1,128)S(1)}, u32[]{:S(2)}, u32[]{:S(2)}) async-start(f32[256,1,640]{2,1,0:T(1,128)} %bitcast.10), calls=%async_computation.1 | async-start | bytes 1310720 | tf_op jit(solution)/shard_map/all_to_all | solution.py:517
  60.1 3.3 %collective-permute-start.6 = (f32[16,8,128]{2,1,0:T(8,128)S(1)}, f32[16,8,128]{2,1,0:T(8,128)S(1)}, u32[]{:S(2)}, u32[]{:S(2)}) collective-permute-start(f32[16,8,128]{2,1,0:T(8,128)S(1)} %get-tuple-element.32), channel_id=1, source_target_pairs={{0,8},{8,16},{16,24},{1,9},{9,17},{17,25},{2,10},{10,18},{18,26},{... | collective-permute-start | bytes 196616 | tf_op jit(solution)/shard_map/ppermute | solution.py:513
  63.4 1.3 %collective-permute-start.7 = (f32[16,8,128]{2,1,0:T(8,128)S(1)}, f32[16,8,128]{2,1,0:T(8,128)S(1)}, u32[]{:S(2)}, u32[]{:S(2)}) collective-permute-start(f32[16,8,128]{2,1,0:T(8,128)S(1)} %get-tuple-element.33), channel_id=1, source_target_pairs={{8,0},{16,8},{24,16},{9,1},{17,9},{25,17},{10,2},{18,10},{26,18},{... | collective-permute-start | bytes 196616 | tf_op jit(solution)/shard_map/ppermute | solution.py:513
  64.7 3.3 %collective-permute-start.4 = (f32[2,16,128]{2,1,0:T(8,128)S(1)}, f32[2,16,128]{2,1,0:T(8,128)S(1)}, u32[]{:S(2)}, u32[]{:S(2)}) collective-permute-start(f32[2,16,128]{2,1,0:T(8,128)S(1)} %get-tuple-element.30), channel_id=1, source_target_pairs={{0,32},{32,64},{64,96},{96,128},{128,160},{160,192},{192,224},{1,3... | collective-permute-start | bytes 49160 | tf_op jit(solution)/shard_map/ppermute | solution.py:513
  68.0 1.3 %collective-permute-start.5 = (f32[2,16,128]{2,1,0:T(8,128)S(1)}, f32[2,16,128]{2,1,0:T(8,128)S(1)}, u32[]{:S(2)}, u32[]{:S(2)}) collective-permute-start(f32[2,16,128]{2,1,0:T(8,128)S(1)} %get-tuple-element.31), channel_id=1, source_target_pairs={{32,0},{64,32},{96,64},{128,96},{160,128},{192,160},{224,192},{33,... | collective-permute-start | bytes 49160 | tf_op jit(solution)/shard_map/ppermute | solution.py:513
  69.3 6.0 %collective-permute-done.5.xp = f32[2,16,128]{2,1,0:T(8,128)S(1)} collective-permute-done((f32[2,16,128]{2,1,0:T(8,128)S(1)}, f32[2,16,128]{2,1,0:T(8,128)S(1)}, u32[]{:S(2)}, u32[]{:S(2)}) %collective-permute-start.5) | collective-permute-done | bytes 16416 | tf_op jit(solution)/shard_map/ppermute | solution.py:513
  75.3 8.0 %all-to-all-done.1 = f32[256,1,640]{2,1,0:T(1,128)S(1)} async-done(((f32[256,1,640]{2,1,0:T(1,128)}), f32[256,1,640]{2,1,0:T(1,128)S(1)}, u32[]{:S(2)}, u32[]{:S(2)}) %all-to-all-start.1) | async-done | bytes 655392 | tf_op jit(solution)/shard_map/all_to_all | solution.py:517
  83.4 5.3 %third.1 = (f32[19,16,16,128]{3,2,1,0:T(8,128)}, f32[3,16,16,128]{3,2,1,0:T(8,128)}, f32[3,512]{1,0:T(4,128)}) custom-call(s32[3]{0:T(128)S(1)} %copy-done.6, f32[19,16,16,128]{3,2,1,0:T(8,128)} %get-tuple-element.29.s2, f32[2,16,128]{2,1,0:T(8,128)S(1)} %collective-permute-done.4.xm, ...), custom_call_target="tpu_custom_call", output_to_operand_aliasing={{0}: (1, {})} | custom-call | tf_op jit(solution)/shard_map/third/pallas_call | solution.py:606
  (31 shorter events, 0.1 us)
Async XLA Ops:
  0.6 45.1 %copy-start.12 = (f32[17]{0:T(128)S(1)}, f32[17]{0:T(128)}, u32[]{:S(2)}) copy-start(f32[17]{0:T(128)} %rev_ref.3) | copy-start | bytes 208
  0.6 45.1 %copy-start.11 = (f32[17]{0:T(128)S(1)}, f32[17]{0:T(128)}, u32[]{:S(2)}) copy-start(f32[17]{0:T(128)} %cond_ref.3) | copy-start | bytes 208
  0.7 45.1 %copy-start.10 = (f32[17]{0:T(128)S(1)}, f32[17]{0:T(128)}, u32[]{:S(2)}) copy-start(f32[17]{0:T(128)} %tau_ref.3) | copy-start | bytes 208
  0.7 45.1 %copy-start.9 = (f32[17]{0:T(128)S(1)}, f32[17]{0:T(128)}, u32[]{:S(2)}) copy-start(f32[17]{0:T(128)} %slope_ref.3) | copy-start | bytes 208
  0.7 45.1 %copy-start.8 = (f32[17]{0:T(128)S(1)}, f32[17]{0:T(128)}, u32[]{:S(2)}) copy-start(f32[17]{0:T(128)} %half_ref.3) | copy-start | bytes 208
  0.7 31.2 %copy-start.7 = (f32[2,64]{1,0:T(2,128)S(1)}, f32[2,64]{1,0:T(2,128)}, u32[]{:S(2)}) copy-start(f32[2,64]{1,0:T(2,128)} %angle.3) | copy-start | bytes 1540
  0.7 31.2 %copy-start.2 = (s32[8,256]{1,0:T(8,128)S(1)}, s32[8,256]{1,0:T(8,128)}, u32[]{:S(2)}) copy-start(s32[8,256]{1,0:T(8,128)} %elem_node.3) | copy-start | bytes 24580
  0.7 31.2 %copy-start.14 = (f32[3]{0:T(128)S(1)}, f32[3]{0:T(128)}, u32[]{:S(2)}) copy-start(f32[3]{0:T(128)} %material.1) | copy-start | bytes 40
  0.7 31.2 %copy-start.13 = (s32[256]{0:T(256)S(1)}, s32[256]{0:T(256)}, u32[]{:S(2)}) copy-start(s32[256]{0:T(256)} %param.31) | copy-start | bytes 3076
  0.7 31.2 %copy-start.5 = (f32[3,512]{1,0:T(4,128)S(1)}, f32[3,512]{1,0:T(4,128)}, u32[]{:S(2)}) copy-start(f32[3,512]{1,0:T(4,128)} %node_disp.1) | copy-start | bytes 18436
  0.7 45.1 %copy-start.3 = (f32[8,8,4]{1,2,0:T(4,128)S(1)}, f32[8,8,4]{1,2,0:T(4,128)}, u32[]{:S(2)}) copy-start(f32[8,8,4]{1,2,0:T(4,128)} %param.28) | copy-start | bytes 3076
  1.3 44.5 %copy-start.6 = (s32[3]{0:T(128)S(1)}, s32[3]{0:T(128)}, u32[]{:S(2)}) copy-start(s32[3]{0:T(128)} %pad_add_fusion.pos_ref) | copy-start | bytes 40
  6.8 38.9 %all-to-all-start = ((f32[256,1,640]{2,1,0:T(1,128)}), f32[256,1,640]{2,1,0:T(1,128)S(1)}, u32[]{:S(2)}, u32[]{:S(2)}) async-start(f32[256,1,640]{2,1,0:T(1,128)} %bitcast.16), calls=%async_computation | async-start | bytes 1310720 | tf_op jit(solution)/shard_map/all_to_all | solution.py:517
  22.5 60.9 %copy-start = (bf16[2,256,512]{2,1,0:T(8,128)(2,1)S(1)}, bf16[2,256,512]{2,1,0:T(8,128)(2,1)}, u32[]{:S(2)}) copy-start(bf16[2,256,512]{2,1,0:T(8,128)(2,1)} %constant.14.clone.blend_hbm) | copy-start | bytes 1572868
  22.5 60.9 %copy-start.1 = (f32[256,128]{1,0:T(8,128)S(1)}, f32[256,128]{1,0:T(8,128)}, u32[]{:S(2)}) copy-start(f32[256,128]{1,0:T(8,128)} %get-tuple-element.36.code_col) | copy-start | bytes 393220
  22.5 15.2 %collective-permute-start.2 = (f32[16,8,128]{2,1,0:T(8,128)}, f32[16,8,128]{2,1,0:T(8,128)S(1)}, u32[]{:S(2)}, u32[]{:S(2)}) collective-permute-start(f32[16,8,128]{2,1,0:T(8,128)} %get-tuple-element.24), channel_id=1, source_target_pairs={{0,8},{8,16},{16,24},{1,9},{9,17},{17,25},{2,10},{10,18},{18,26},{... | collective-permute-start | bytes 196616 | tf_op jit(solution)/shard_map/ppermute | solution.py:513
  26.0 11.8 %collective-permute-start.3 = (f32[16,8,128]{2,1,0:T(8,128)}, f32[16,8,128]{2,1,0:T(8,128)S(1)}, u32[]{:S(2)}, u32[]{:S(2)}) collective-permute-start(f32[16,8,128]{2,1,0:T(8,128)} %get-tuple-element.25), channel_id=1, source_target_pairs={{8,0},{16,8},{24,16},{9,1},{17,9},{25,17},{10,2},{18,10},{26,18},{... | collective-permute-start | bytes 196616 | tf_op jit(solution)/shard_map/ppermute | solution.py:513
  27.3 6.4 %collective-permute-start = (f32[2,16,128]{2,1,0:T(8,128)}, f32[2,16,128]{2,1,0:T(8,128)S(1)}, u32[]{:S(2)}, u32[]{:S(2)}) collective-permute-start(f32[2,16,128]{2,1,0:T(8,128)} %get-tuple-element.22), channel_id=1, source_target_pairs={{0,32},{32,64},{64,96},{96,128},{128,160},{160,192},{192,224},{1,3... | collective-permute-start | bytes 49160 | tf_op jit(solution)/shard_map/ppermute | solution.py:513
  30.6 7.2 %collective-permute-start.1 = (f32[2,16,128]{2,1,0:T(8,128)}, f32[2,16,128]{2,1,0:T(8,128)S(1)}, u32[]{:S(2)}, u32[]{:S(2)}) collective-permute-start(f32[2,16,128]{2,1,0:T(8,128)} %get-tuple-element.23), channel_id=1, source_target_pairs={{32,0},{64,32},{96,64},{128,96},{160,128},{192,160},{224,192},{33,... | collective-permute-start | bytes 49160 | tf_op jit(solution)/shard_map/ppermute | solution.py:513
  53.7 29.6 %all-to-all-start.1 = ((f32[256,1,640]{2,1,0:T(1,128)}), f32[256,1,640]{2,1,0:T(1,128)S(1)}, u32[]{:S(2)}, u32[]{:S(2)}) async-start(f32[256,1,640]{2,1,0:T(1,128)} %bitcast.10), calls=%async_computation.1 | async-start | bytes 1310720 | tf_op jit(solution)/shard_map/all_to_all | solution.py:517
  60.1 15.2 %collective-permute-start.6 = (f32[16,8,128]{2,1,0:T(8,128)S(1)}, f32[16,8,128]{2,1,0:T(8,128)S(1)}, u32[]{:S(2)}, u32[]{:S(2)}) collective-permute-start(f32[16,8,128]{2,1,0:T(8,128)S(1)} %get-tuple-element.32), channel_id=1, source_target_pairs={{0,8},{8,16},{16,24},{1,9},{9,17},{17,25},{2,10},{10,18},{18,26},{... | collective-permute-start | bytes 196616 | tf_op jit(solution)/shard_map/ppermute | solution.py:513
  63.4 11.9 %collective-permute-start.7 = (f32[16,8,128]{2,1,0:T(8,128)S(1)}, f32[16,8,128]{2,1,0:T(8,128)S(1)}, u32[]{:S(2)}, u32[]{:S(2)}) collective-permute-start(f32[16,8,128]{2,1,0:T(8,128)S(1)} %get-tuple-element.33), channel_id=1, source_target_pairs={{8,0},{16,8},{24,16},{9,1},{17,9},{25,17},{10,2},{18,10},{26,18},{... | collective-permute-start | bytes 196616 | tf_op jit(solution)/shard_map/ppermute | solution.py:513
  64.7 4.6 %collective-permute-start.4 = (f32[2,16,128]{2,1,0:T(8,128)S(1)}, f32[2,16,128]{2,1,0:T(8,128)S(1)}, u32[]{:S(2)}, u32[]{:S(2)}) collective-permute-start(f32[2,16,128]{2,1,0:T(8,128)S(1)} %get-tuple-element.30), channel_id=1, source_target_pairs={{0,32},{32,64},{64,96},{96,128},{128,160},{160,192},{192,224},{1,3... | collective-permute-start | bytes 49160 | tf_op jit(solution)/shard_map/ppermute | solution.py:513
  68.0 7.3 %collective-permute-start.5 = (f32[2,16,128]{2,1,0:T(8,128)S(1)}, f32[2,16,128]{2,1,0:T(8,128)S(1)}, u32[]{:S(2)}, u32[]{:S(2)}) collective-permute-start(f32[2,16,128]{2,1,0:T(8,128)S(1)} %get-tuple-element.31), channel_id=1, source_target_pairs={{32,0},{64,32},{96,64},{128,96},{160,128},{192,160},{224,192},{33,... | collective-permute-start | bytes 49160 | tf_op jit(solution)/shard_map/ppermute | solution.py:513
  (1 other events, 0.7 us)

commit v3 on v2

--- a/solution.py
+++ b/solution.py
@@ -22,6 +22,10 @@
 
 def iota(shape, dim):
     return lax.broadcasted_iota(jnp.int32, shape, dim)
+
+
+def place():
+    return [lax.axis_index(a) for a in ALL]
 
 
 def neighbour(pos_ref, sizes, step):
@@ -137,8 +141,10 @@
 def send_faces(v, pos_ref, sizes, xlo, xhi, ylo, yhi, msg, lines):
     xlo[...] = v[0:2]
     xhi[...] = v[14:16]
-    ylo[...] = v[:, 0:8, :]
-    yhi[...] = v[:, 8:16, :]
+    for x in range(CX):
+        for n in range(2):
+            ylo[n, x : x + 1] = v[x, n : n + 1, :]
+            yhi[n, x : x + 1] = v[x, 14 + n : 15 + n, :]
     row, lane = iota((8, 128), 0), iota((8, 128), 1)
     pick = ((row < 4) & (lane == jnp.where(row < 2, row, row + 124))).astype(F32)
     flat = v[...].reshape(CX * CY, CZ)
@@ -150,9 +156,8 @@
             put_row(msg, peer, ok, ends[k : k + 1, 128 * half : 128 * half + 128], 1 + n)
     lines[0:16] = v[0]
     lines[16:32] = v[15]
-    for x in range(CX):
-        lines[32 + x : 33 + x] = v[x, 0:1, :]
-        lines[48 + x : 49 + x] = v[x, 15:16, :]
+    lines[32:48] = ylo[0]
+    lines[48:64] = yhi[1]
     lines[64:128] = jnp.zeros((64, 128), F32)
     marks = lax.dot_general(pick, lines[...], NT, precision=HIGHEST, preferred_element_type=F32)
     for dx in (-1, 1):
@@ -213,8 +218,10 @@
     vext[2:18, 8:24, 0:128] = v[...]
     vext[0:2, 8:24, 0:128] = xm[...]
     vext[18:20, 8:24, 0:128] = xp[...]
-    vext[2:18, 0:8, 0:128] = ym[...]
-    vext[2:18, 24:32, 0:128] = yp[...]
+    for x in range(CX):
+        for n in range(2):
+            vext[2 + x, 6 + n : 7 + n, 0:128] = ym[n, x : x + 1]
+            vext[2 + x, 24 + n : 25 + n, 0:128] = yp[n, x : x + 1]
     row, lane = iota((8, 128), 0), iota((8, 128), 1)
     place = ((row < 4) & (lane == jnp.where(row < 2, row + 126, row - 2))).astype(F32)
     outer = []
@@ -288,8 +295,9 @@
     return jnp.sum(jnp.where(iota((256, 256), 0) == iota((256, 256), 1), wide, 0.0), axis=0, keepdims=True)
 
 
-def first_kernel(sizes, pos_ref, act_ref, fi_ref, half_ref, slope_ref, tau_ref, cond_ref, rev_ref, angle, conduct, block_elem,
-                 states_hbm, s1_hbm, xlo, xhi, ylo, yhi, msg, code_col, code_row, const, lines, states, s1, came, left, total, moment):
+def first_kernel(sizes, act_ref, fi_ref, half_ref, slope_ref, tau_ref, cond_ref, rev_ref, angle, conduct, block_elem,
+                 states_hbm, s1_hbm, xlo, xhi, ylo, yhi, msg, code_col, const, lines, states, s1, came, left, total, moment):
+    pos_ref = place()
     coming = fetches(states_hbm, states, came)
     gate_constants(half_ref, slope_ref, tau_ref, cond_ref, rev_ref, const)
     ids = blocks(block_elem)
@@ -301,7 +309,6 @@
     code = owner + 256.0 * rank
     code_col[...] = code[:, 0:128]
     row_code = to_row(code)
-    code_row[...] = jnp.broadcast_to(row_code, (8, 256))
     local_row = to_row(local) + 1.0
     peers = iota((256, 256), 0).astype(F32)
     lane = iota((1, 128), 1)
@@ -381,9 +388,10 @@
     passive[...] = total[0:8] + total[8:16] + total[16:24]
 
 
-def second_kernel(sizes, pos_ref, half_ref, slope_ref, tau_ref, cond_ref, rev_ref, s1_hbm, xm, xp, ym, yp, got1, corner,
-                  code_row, block_weight, s2_hbm, xlo, xhi, ylo, yhi, msg, heard, const, lines, s1, s2, came, left, total, moment, vext, fx, cx, cy, cz,
+def second_kernel(sizes, half_ref, slope_ref, tau_ref, cond_ref, rev_ref, s1_hbm, xm, xp, ym, yp, got1, corner,
+                  code_col, block_weight, s2_hbm, xlo, xhi, ylo, yhi, msg, heard, const, lines, s1, s2, came, left, total, moment, vext, fx, cx, cy, cz,
                   tens):
+    pos_ref = place()
     coming = fetches(s1_hbm, s1, came)
     gate_constants(half_ref, slope_ref, tau_ref, cond_ref, rev_ref, const)
     heard[...] = got1[FIRST, :]
@@ -414,12 +422,13 @@
     value = to_row(column_wide(mean[:, 0:4] * blocks(block_weight)))
     peers = iota((256, 256), 0).astype(F32)
     elems = iota((256, 256), 1).astype(F32)
+    row_code = to_row(jnp.concatenate([code_col[...], code_col[...]], 1))
     target = iota((128, 256), 0)
     answer = jnp.zeros((256, 128), F32)
     asked = heard[...]
     none = jnp.zeros((64, 256), F32)
     for r in range(2):
-        goes = (code_row[0:1, :] == peers + 256.0 * r).astype(F32).astype(BF16)
+        goes = (row_code == peers + 256.0 * r).astype(F32).astype(BF16)
         for part in parts3(jnp.where(target == 64 * r + 3, value, 0.0)):
             answer += lax.dot_general(goes, part, NT, preferred_element_type=F32)
         wants = (asked[:, r : r + 1] == elems + 1.0).astype(F32).astype(BF16)
@@ -433,8 +442,9 @@
         copy.wait()
 
 
-def third_kernel(sizes, pos_ref, s2, xm, xp, ym, yp, heard, got2, code_col, elem_node, passive, active, blend_hbm, s3, fine,
+def third_kernel(sizes, s2, xm, xp, ym, yp, heard, got2, code_col, elem_node, passive, active, blend_hbm, s3, fine,
                  residual, vext, fx, cx, cy, cz, blend, came):
+    pos_ref = place()
     coming = pltpu.make_async_copy(blend_hbm, blend, came)
     coming.start()
     live = tile_planes(pos_ref, sizes, heard, cx, cy, cz)
@@ -544,7 +554,7 @@
     return jax.ShapeDtypeStruct(shape, F32)
 
 
-FACES = [sds(2, 16, 128), sds(2, 16, 128), sds(16, 8, 128), sds(16, 8, 128), sds(ROWS * 256, 128)]
+FACES = [sds(2, 16, 128), sds(2, 16, 128), sds(2, 16, 128), sds(2, 16, 128), sds(ROWS * 256, 128)]
 STEP_SCRATCH = [
     pltpu.VMEM((20, 32, 256), F32),
     pltpu.VMEM((18, 16, 128), F32),
@@ -568,15 +578,14 @@
 def shards(states, active, fibre_index, fibre_angle, conduct, gate_half, gate_slope, gate_tau, conductance, reversal,
            block_elem, block_weight, node_disp, elem_node, elem_fibre, material):
     sizes = tuple(lax.axis_size(a) for a in ALL)
-    pos = jnp.stack([lax.axis_index(a) for a in ALL]).astype(jnp.int32)
     gates = (gate_half, gate_slope, gate_tau, conductance, reversal)
     full = sds(NSTATE, CX, CY, CZ)
-    s1, *faces, code_col, code_row = call(
+    s1, *faces, code_col = call(
         functools.partial(first_kernel, sizes),
         "first",
-        (pos, active.reshape(2), fibre_index.reshape(2), *gates),
+        (active.reshape(2), fibre_index.reshape(2), *gates),
         (fibre_angle, conduct, block_elem.transpose(0, 2, 1), states),
-        [full, *FACES, sds(256, 128), sds(8, 256)],
+        [full, *FACES, sds(256, 128)],
         GATE_SCRATCH + STATE_SCRATCH,
         (3, 4),
         60,
@@ -592,8 +601,8 @@
     s2, *faces, heard = call(
         functools.partial(second_kernel, sizes),
         "second",
-        (pos, *gates),
-        (s1, *halo, got1, corner, code_row, block_weight.transpose(0, 2, 1)),
+        gates,
+        (s1, *halo, got1, corner, code_col, block_weight.transpose(0, 2, 1)),
         [full, *FACES, sds(256, 128)],
         GATE_SCRATCH + STATE_SCRATCH + STEP_SCRATCH + [pltpu.VMEM((16, 16, 128), F32)],
         (0, 9),
@@ -607,13 +616,13 @@
         functools.partial(third_kernel, sizes),
         grid=(1,),
         out_shape=outs,
-        in_specs=[whole((3,), pltpu.SMEM), plane, *[whole(x.shape) for x in rest], ANYWHERE],
+        in_specs=[plane, *[whole(x.shape) for x in rest], ANYWHERE],
         out_specs=[plane, whole(outs[1].shape), whole(outs[2].shape)],
         scratch_shapes=STEP_SCRATCH + [pltpu.VMEM(blend.shape, BF16), pltpu.SemaphoreType.DMA],
-        input_output_aliases={1: 0},
+        input_output_aliases={0: 0},
         compiler_params=grant(50),
         name="third",
-    )(pos, s2, *rest, blend)
+    )(s2, *rest, blend)
 
 
 def solution(mesh):

time: 89.2 us -> 88.6 us (level)
  no operation moved by 1% of the time
where the time goes in v3:
time: 88.6 us; the launch traced here: 88.1 us
  starting transfers between devices  40.3 us (45%)
  waiting for transfers between devices  26.3 us (30%)
  Pallas kernels  19.6 us (22%)
  local copies, waits for them, and re-layouts  0.96 us (1%)
  between operations  0.93 us (1%)
    all_to_all x2, starting transfers between devices, exchange(): lax.all_to_all(msg.reshape(256, 1, ROWS * 128), ALL, 0, 0, tiled=True)  21.9 us
    ppermute x8, starting transfers between devices, shift(): return lax.ppermute(x, axis, pairs)  18.4 us
    all_to_all x2, waiting for transfers between devices, exchange(): lax.all_to_all(msg.reshape(256, 1, ROWS * 128), ALL, 0, 0, tiled=True)  16.1 us
    pallas_call x3, Pallas kernels, call(): pl.pallas_call(body, grid=(1,), out_shape=outs, in_specs=[whole(x.shape,...  14.3 us
    ppermute x8, waiting for transfers between devices, shift(): return lax.ppermute(x, axis, pairs)  10.2 us
    pallas_call x1, Pallas kernels, shards(): pl.pallas_call(functools.partial(third_kernel, sizes), grid=(1,), out_sha...  5.27 us
  transfers between devices with their start and end apart: 10, of which 4 were waited for; matrix products, arithmetic and copies ran while one was open for 0% of the time, Pallas kernels for 2%

profile of v3, /device:TPU:1, one launch (start us, length us, event | category | flops | bytes accessed | tf_op | source)
XLA Modules:
  0.0 88.1 jit_solution(12878566492597977906)
XLA Ops:
  0.7 5.4 %first.1 = (f32[19,16,16,128]{3,2,1,0:T(8,128)}, f32[2,16,128]{2,1,0:T(8,128)}, f32[2,16,128]{2,1,0:T(8,128)}, f32[2,16,128]{2,1,0:T(8,128)}, f32[2,16,128]{2,1,...) custom-call(s32[2]{0:T(128)} %bitcast.15, s32[2]{0:T(128)} %bitcast.16, f32[17]{0:T(128)} %half_ref.3, f32[17]{0:T(128)} %slope_ref.3, ...), custom_call_target="tpu_custom_call" | custom-call | tf_op jit(solution)/shard_map/first/pallas_call | solution.py:541
  6.2 0.0 copy-start.1
  6.2 0.0 copy-start.2
  6.2 15.7 %all-to-all-start = ((f32[256,1,640]{2,1,0:T(1,128)}), f32[256,1,640]{2,1,0:T(1,128)S(1)}, u32[]{:S(2)}, u32[]{:S(2)}) async-start(f32[256,1,640]{2,1,0:T(1,128)} %bitcast.13), calls=%async_computation | async-start | bytes 1310720 | tf_op jit(solution)/shard_map/all_to_all | solution.py:527
  21.8 3.4 %collective-permute-start = (f32[2,16,128]{2,1,0:T(8,128)}, f32[2,16,128]{2,1,0:T(8,128)S(1)}, u32[]{:S(2)}, u32[]{:S(2)}) collective-permute-start(f32[2,16,128]{2,1,0:T(8,128)} %get-tuple-element.21), channel_id=1, source_target_pairs={{0,32},{32,64},{64,96},{96,128},{128,160},{160,192},{192,224},{1,3... | collective-permute-start | bytes 49160 | tf_op jit(solution)/shard_map/ppermute | solution.py:523
  25.3 1.3 %collective-permute-start.1 = (f32[2,16,128]{2,1,0:T(8,128)}, f32[2,16,128]{2,1,0:T(8,128)S(1)}, u32[]{:S(2)}, u32[]{:S(2)}) collective-permute-start(f32[2,16,128]{2,1,0:T(8,128)} %get-tuple-element.22), channel_id=1, source_target_pairs={{32,0},{64,32},{96,64},{128,96},{160,128},{192,160},{224,192},{33,... | collective-permute-start | bytes 49160 | tf_op jit(solution)/shard_map/ppermute | solution.py:523
  26.6 3.2 %collective-permute-start.2 = (f32[2,16,128]{2,1,0:T(8,128)}, f32[2,16,128]{2,1,0:T(8,128)S(1)}, u32[]{:S(2)}, u32[]{:S(2)}) collective-permute-start(f32[2,16,128]{2,1,0:T(8,128)} %get-tuple-element.23), channel_id=1, source_target_pairs={{0,8},{8,16},{16,24},{1,9},{9,17},{17,25},{2,10},{10,18},{18,26},{... | collective-permute-start | bytes 49160 | tf_op jit(solution)/shard_map/ppermute | solution.py:523
  29.7 1.3 %collective-permute-start.3 = (f32[2,16,128]{2,1,0:T(8,128)}, f32[2,16,128]{2,1,0:T(8,128)S(1)}, u32[]{:S(2)}, u32[]{:S(2)}) collective-permute-start(f32[2,16,128]{2,1,0:T(8,128)} %get-tuple-element.24), channel_id=1, source_target_pairs={{8,0},{16,8},{24,16},{9,1},{17,9},{25,17},{10,2},{18,10},{26,18},{... | collective-permute-start | bytes 49160 | tf_op jit(solution)/shard_map/ppermute | solution.py:523
  31.1 1.8 %elements.1 = (f32[64,256]{1,0:T(8,128)S(1)}, f32[8,512]{1,0:T(8,128)S(1)}, f32[64,256]{1,0:T(8,128)S(1)}) custom-call(f32[3]{0:T(128)S(1)} %copy-done.13, f32[2,64]{1,0:T(2,128)S(1)} %copy-done.6, f32[3,512]{1,0:T(4,128)S(1)} %copy-done.5, s32[8,256]{1,0:T(8,128)S(1)} %copy-done.3, s32[1,256]{1,0:T(1,128)S(1)} %bitcast.12), custom_call_target="tpu_custom_call" | custom-call | tf_op jit(solution)/shard_map/elements/pallas_call | solution.py:541
  32.8 0.0 collective-permute-done.xm
  32.9 4.2 %collective-permute-done.1.xp = f32[2,16,128]{2,1,0:T(8,128)S(1)} collective-permute-done((f32[2,16,128]{2,1,0:T(8,128)}, f32[2,16,128]{2,1,0:T(8,128)S(1)}, u32[]{:S(2)}, u32[]{:S(2)}) %collective-permute-start.1) | collective-permute-done | bytes 16416 | tf_op jit(solution)/shard_map/ppermute | solution.py:523
  37.1 8.1 %all-to-all-done = f32[256,1,640]{2,1,0:T(1,128)S(1)} async-done(((f32[256,1,640]{2,1,0:T(1,128)}), f32[256,1,640]{2,1,0:T(1,128)S(1)}, u32[]{:S(2)}, u32[]{:S(2)}) %all-to-all-start) | async-done | bytes 655392 | tf_op jit(solution)/shard_map/all_to_all | solution.py:527
  45.2 0.0 copy-start
  45.2 0.9 %copy-done = f32[256,128]{1,0:T(8,128)S(1)} copy-done((f32[256,128]{1,0:T(8,128)S(1)}, f32[256,128]{1,0:T(8,128)}, u32[]{:S(2)}) %copy-start) | copy-done | bytes 131096
  46.1 7.1 %second.1 = (f32[19,16,16,128]{3,2,1,0:T(8,128)}, f32[2,16,128]{2,1,0:T(8,128)S(1)}, f32[2,16,128]{2,1,0:T(8,128)S(1)}, f32[2,16,128]{2,1,0:T(8,128)S(1)}, f32[2...) custom-call(f32[17]{0:T(128)S(1)} %copy-done.7, f32[17]{0:T(128)S(1)} %copy-done.8, ...), custom_call_target="tpu_custom_call" | custom-call | tf_op jit(solution)/shard_map/second/pallas_call | solution.py:541
  53.2 6.2 %all-to-all-start.1 = ((f32[256,1,640]{2,1,0:T(1,128)}), f32[256,1,640]{2,1,0:T(1,128)S(1)}, u32[]{:S(2)}, u32[]{:S(2)}) async-start(f32[256,1,640]{2,1,0:T(1,128)} %bitcast.7), calls=%async_computation.1 | async-start | bytes 1310720 | tf_op jit(solution)/shard_map/all_to_all | solution.py:527
  59.4 3.5 %collective-permute-start.4 = (f32[2,16,128]{2,1,0:T(8,128)S(1)}, f32[2,16,128]{2,1,0:T(8,128)S(1)}, u32[]{:S(2)}, u32[]{:S(2)}) collective-permute-start(f32[2,16,128]{2,1,0:T(8,128)S(1)} %get-tuple-element.29), channel_id=1, source_target_pairs={{0,32},{32,64},{64,96},{96,128},{128,160},{160,192},{192,224},{1,3... | collective-permute-start | bytes 49160 | tf_op jit(solution)/shard_map/ppermute | solution.py:523
  63.0 1.3 %collective-permute-start.5 = (f32[2,16,128]{2,1,0:T(8,128)S(1)}, f32[2,16,128]{2,1,0:T(8,128)S(1)}, u32[]{:S(2)}, u32[]{:S(2)}) collective-permute-start(f32[2,16,128]{2,1,0:T(8,128)S(1)} %get-tuple-element.30), channel_id=1, source_target_pairs={{32,0},{64,32},{96,64},{128,96},{160,128},{192,160},{224,192},{33,... | collective-permute-start | bytes 49160 | tf_op jit(solution)/shard_map/ppermute | solution.py:523
  64.3 3.2 %collective-permute-start.6 = (f32[2,16,128]{2,1,0:T(8,128)S(1)}, f32[2,16,128]{2,1,0:T(8,128)S(1)}, u32[]{:S(2)}, u32[]{:S(2)}) collective-permute-start(f32[2,16,128]{2,1,0:T(8,128)S(1)} %get-tuple-element.31), channel_id=1, source_target_pairs={{0,8},{8,16},{16,24},{1,9},{9,17},{17,25},{2,10},{10,18},{18,26},{... | collective-permute-start | bytes 49160 | tf_op jit(solution)/shard_map/ppermute | solution.py:523
  67.4 1.3 %collective-permute-start.7 = (f32[2,16,128]{2,1,0:T(8,128)S(1)}, f32[2,16,128]{2,1,0:T(8,128)S(1)}, u32[]{:S(2)}, u32[]{:S(2)}) collective-permute-start(f32[2,16,128]{2,1,0:T(8,128)S(1)} %get-tuple-element.32), channel_id=1, source_target_pairs={{8,0},{16,8},{24,16},{9,1},{17,9},{25,17},{10,2},{18,10},{26,18},{... | collective-permute-start | bytes 49160 | tf_op jit(solution)/shard_map/ppermute | solution.py:523
  68.7 0.0 collective-permute-done.4.xm
  68.7 6.0 %collective-permute-done.5.xp = f32[2,16,128]{2,1,0:T(8,128)S(1)} collective-permute-done((f32[2,16,128]{2,1,0:T(8,128)S(1)}, f32[2,16,128]{2,1,0:T(8,128)S(1)}, u32[]{:S(2)}, u32[]{:S(2)}) %collective-permute-start.5) | collective-permute-done | bytes 16416 | tf_op jit(solution)/shard_map/ppermute | solution.py:523
  74.7 8.1 %all-to-all-done.1 = f32[256,1,640]{2,1,0:T(1,128)S(1)} async-done(((f32[256,1,640]{2,1,0:T(1,128)}), f32[256,1,640]{2,1,0:T(1,128)S(1)}, u32[]{:S(2)}, u32[]{:S(2)}) %all-to-all-start.1) | async-done | bytes 655392 | tf_op jit(solution)/shard_map/all_to_all | solution.py:527
  82.8 5.3 %third.1 = (f32[19,16,16,128]{3,2,1,0:T(8,128)}, f32[3,16,16,128]{3,2,1,0:T(8,128)}, f32[3,512]{1,0:T(4,128)}) custom-call(f32[19,16,16,128]{3,2,1,0:T(8,128)} %get-tuple-element.28.s2, f32[2,16,128]{2,1,0:T(8,128)S(1)} %collective-permute-done.4.xm, f32[2,16,128]{2,1,0:T(8,128)S(1)} %collective-permute-done.5.xp, ...), custom_call_target="tpu_custom_call", output_to_operand_aliasing={{0}: (0, {})} | custom-call | tf_op jit(solution)/shard_map/third/pallas_call | solution.py:615
  (28 shorter events, 0.1 us)
Async XLA Ops:
  0.6 44.5 %copy-start.11 = (f32[17]{0:T(128)S(1)}, f32[17]{0:T(128)}, u32[]{:S(2)}) copy-start(f32[17]{0:T(128)} %rev_ref.3) | copy-start | bytes 208
  0.6 44.5 %copy-start.10 = (f32[17]{0:T(128)S(1)}, f32[17]{0:T(128)}, u32[]{:S(2)}) copy-start(f32[17]{0:T(128)} %cond_ref.3) | copy-start | bytes 208
  0.7 44.5 %copy-start.9 = (f32[17]{0:T(128)S(1)}, f32[17]{0:T(128)}, u32[]{:S(2)}) copy-start(f32[17]{0:T(128)} %tau_ref.3) | copy-start | bytes 208
  0.7 44.5 %copy-start.8 = (f32[17]{0:T(128)S(1)}, f32[17]{0:T(128)}, u32[]{:S(2)}) copy-start(f32[17]{0:T(128)} %slope_ref.3) | copy-start | bytes 208
  0.7 44.5 %copy-start.7 = (f32[17]{0:T(128)S(1)}, f32[17]{0:T(128)}, u32[]{:S(2)}) copy-start(f32[17]{0:T(128)} %half_ref.3) | copy-start | bytes 208
  0.7 30.3 %copy-start.6 = (f32[2,64]{1,0:T(2,128)S(1)}, f32[2,64]{1,0:T(2,128)}, u32[]{:S(2)}) copy-start(f32[2,64]{1,0:T(2,128)} %angle.3) | copy-start | bytes 1540
  0.7 30.3 %copy-start.3 = (s32[8,256]{1,0:T(8,128)S(1)}, s32[8,256]{1,0:T(8,128)}, u32[]{:S(2)}) copy-start(s32[8,256]{1,0:T(8,128)} %elem_node.3) | copy-start | bytes 24580
  0.7 30.3 %copy-start.13 = (f32[3]{0:T(128)S(1)}, f32[3]{0:T(128)}, u32[]{:S(2)}) copy-start(f32[3]{0:T(128)} %material.1) | copy-start | bytes 40
  0.7 30.3 %copy-start.12 = (s32[256]{0:T(256)S(1)}, s32[256]{0:T(256)}, u32[]{:S(2)}) copy-start(s32[256]{0:T(256)} %param.31) | copy-start | bytes 3076
  0.7 30.3 %copy-start.5 = (f32[3,512]{1,0:T(4,128)S(1)}, f32[3,512]{1,0:T(4,128)}, u32[]{:S(2)}) copy-start(f32[3,512]{1,0:T(4,128)} %node_disp.1) | copy-start | bytes 18436
  0.7 44.4 %copy-start.4 = (f32[8,8,4]{1,2,0:T(4,128)S(1)}, f32[8,8,4]{1,2,0:T(4,128)}, u32[]{:S(2)}) copy-start(f32[8,8,4]{1,2,0:T(4,128)} %param.28) | copy-start | bytes 3076
  6.2 76.7 %copy-start.1 = (f32[256,128]{1,0:T(8,128)S(1)}, f32[256,128]{1,0:T(8,128)}, u32[]{:S(2)}) copy-start(f32[256,128]{1,0:T(8,128)} %get-tuple-element.27.code_col) | copy-start | bytes 393220
  6.2 76.7 %copy-start.2 = (bf16[2,256,512]{2,1,0:T(8,128)(2,1)S(1)}, bf16[2,256,512]{2,1,0:T(8,128)(2,1)}, u32[]{:S(2)}) copy-start(bf16[2,256,512]{2,1,0:T(8,128)(2,1)} %constant.2.clone.blend_hbm) | copy-start | bytes 1572868
  6.2 38.9 %all-to-all-start = ((f32[256,1,640]{2,1,0:T(1,128)}), f32[256,1,640]{2,1,0:T(1,128)S(1)}, u32[]{:S(2)}, u32[]{:S(2)}) async-start(f32[256,1,640]{2,1,0:T(1,128)} %bitcast.13), calls=%async_computation | async-start | bytes 1310720 | tf_op jit(solution)/shard_map/all_to_all | solution.py:527
  21.8 11.0 %collective-permute-start = (f32[2,16,128]{2,1,0:T(8,128)}, f32[2,16,128]{2,1,0:T(8,128)S(1)}, u32[]{:S(2)}, u32[]{:S(2)}) collective-permute-start(f32[2,16,128]{2,1,0:T(8,128)} %get-tuple-element.21), channel_id=1, source_target_pairs={{0,32},{32,64},{64,96},{96,128},{128,160},{160,192},{192,224},{1,3... | collective-permute-start | bytes 49160 | tf_op jit(solution)/shard_map/ppermute | solution.py:523
  25.3 11.8 %collective-permute-start.1 = (f32[2,16,128]{2,1,0:T(8,128)}, f32[2,16,128]{2,1,0:T(8,128)S(1)}, u32[]{:S(2)}, u32[]{:S(2)}) collective-permute-start(f32[2,16,128]{2,1,0:T(8,128)} %get-tuple-element.22), channel_id=1, source_target_pairs={{32,0},{64,32},{96,64},{128,96},{160,128},{192,160},{224,192},{33,... | collective-permute-start | bytes 49160 | tf_op jit(solution)/shard_map/ppermute | solution.py:523
  26.6 10.5 %collective-permute-start.2 = (f32[2,16,128]{2,1,0:T(8,128)}, f32[2,16,128]{2,1,0:T(8,128)S(1)}, u32[]{:S(2)}, u32[]{:S(2)}) collective-permute-start(f32[2,16,128]{2,1,0:T(8,128)} %get-tuple-element.23), channel_id=1, source_target_pairs={{0,8},{8,16},{16,24},{1,9},{9,17},{17,25},{2,10},{10,18},{18,26},{... | collective-permute-start | bytes 49160 | tf_op jit(solution)/shard_map/ppermute | solution.py:523
  29.7 7.3 %collective-permute-start.3 = (f32[2,16,128]{2,1,0:T(8,128)}, f32[2,16,128]{2,1,0:T(8,128)S(1)}, u32[]{:S(2)}, u32[]{:S(2)}) collective-permute-start(f32[2,16,128]{2,1,0:T(8,128)} %get-tuple-element.24), channel_id=1, source_target_pairs={{8,0},{16,8},{24,16},{9,1},{17,9},{25,17},{10,2},{18,10},{26,18},{... | collective-permute-start | bytes 49160 | tf_op jit(solution)/shard_map/ppermute | solution.py:523
  45.2 0.9 %copy-start = (f32[256,128]{1,0:T(8,128)S(1)}, f32[256,128]{1,0:T(8,128)}, u32[]{:S(2)}) copy-start(f32[256,128]{1,0:T(8,128)} %get-tuple-element.27.code_col) | copy-start | bytes 393220
  53.2 29.6 %all-to-all-start.1 = ((f32[256,1,640]{2,1,0:T(1,128)}), f32[256,1,640]{2,1,0:T(1,128)S(1)}, u32[]{:S(2)}, u32[]{:S(2)}) async-start(f32[256,1,640]{2,1,0:T(1,128)} %bitcast.7), calls=%async_computation.1 | async-start | bytes 1310720 | tf_op jit(solution)/shard_map/all_to_all | solution.py:527
  59.4 9.3 %collective-permute-start.4 = (f32[2,16,128]{2,1,0:T(8,128)S(1)}, f32[2,16,128]{2,1,0:T(8,128)S(1)}, u32[]{:S(2)}, u32[]{:S(2)}) collective-permute-start(f32[2,16,128]{2,1,0:T(8,128)S(1)} %get-tuple-element.29), channel_id=1, source_target_pairs={{0,32},{32,64},{64,96},{96,128},{128,160},{160,192},{192,224},{1,3... | collective-permute-start | bytes 49160 | tf_op jit(solution)/shard_map/ppermute | solution.py:523
  63.0 11.8 %collective-permute-start.5 = (f32[2,16,128]{2,1,0:T(8,128)S(1)}, f32[2,16,128]{2,1,0:T(8,128)S(1)}, u32[]{:S(2)}, u32[]{:S(2)}) collective-permute-start(f32[2,16,128]{2,1,0:T(8,128)S(1)} %get-tuple-element.30), channel_id=1, source_target_pairs={{32,0},{64,32},{96,64},{128,96},{160,128},{192,160},{224,192},{33,... | collective-permute-start | bytes 49160 | tf_op jit(solution)/shard_map/ppermute | solution.py:523
  64.3 10.5 %collective-permute-start.6 = (f32[2,16,128]{2,1,0:T(8,128)S(1)}, f32[2,16,128]{2,1,0:T(8,128)S(1)}, u32[]{:S(2)}, u32[]{:S(2)}) collective-permute-start(f32[2,16,128]{2,1,0:T(8,128)S(1)} %get-tuple-element.31), channel_id=1, source_target_pairs={{0,8},{8,16},{16,24},{1,9},{9,17},{17,25},{2,10},{10,18},{18,26},{... | collective-permute-start | bytes 49160 | tf_op jit(solution)/shard_map/ppermute | solution.py:523
  67.4 7.3 %collective-permute-start.7 = (f32[2,16,128]{2,1,0:T(8,128)S(1)}, f32[2,16,128]{2,1,0:T(8,128)S(1)}, u32[]{:S(2)}, u32[]{:S(2)}) collective-permute-start(f32[2,16,128]{2,1,0:T(8,128)S(1)} %get-tuple-element.32), channel_id=1, source_target_pairs={{8,0},{16,8},{24,16},{9,1},{17,9},{25,17},{10,2},{18,10},{26,18},{... | collective-permute-start | bytes 49160 | tf_op jit(solution)/shard_map/ppermute | solution.py:523

commit v4 on v3

--- a/solution.py
+++ b/solution.py
@@ -264,7 +264,7 @@
     one(1, 0)
     one(18, 3)
 
-    @pl.loop(2, 18, unroll=4)
+    @pl.loop(2, 18, unroll=8)
     def _(p):
         one(p, jnp.where(p < 10, 1, 2))
 
@@ -400,7 +400,7 @@
     fill_extended(vext, s1.at[0], (xm, xp, ym, yp), got1, pos_ref, sizes)
     flux_x(vext, fx, cx)
 
-    @pl.loop(0, CX, unroll=4)
+    @pl.loop(0, CX, unroll=8)
     def _(x):
         here = jnp.where(x < 8, live[0], live[1])
         tens[x] = s1[0, x] + here * lap_plane(vext, fx, cy, cz, x)
@@ -451,7 +451,7 @@
     fill_extended(vext, s2.at[0], (xm, xp, ym, yp), got2, pos_ref, sizes)
     flux_x(vext, fx, cx)
 
-    @pl.loop(0, CX, unroll=4)
+    @pl.loop(0, CX, unroll=8)
     def _(x):
         here = jnp.where(x < 8, live[0], live[1])
         s3[0, x] = s2[0, x] + here * lap_plane(vext, fx, cy, cz, x)
@@ -462,12 +462,12 @@
     for r in range(2):
         wants = asked[:, r : r + 1] == elems + 1.0
         tension += jnp.sum(jnp.where(wants, answer[:, 64 * r + 3 : 64 * r + 4], 0.0), axis=0, keepdims=True)
-    total = jnp.zeros((24, NODES), F32)
+    total = jnp.zeros((16, NODES), F32)
     for q in range(8):
         hot = (iota((NODES, ELEMS), 0) == elem_node[q : q + 1, :]).astype(F32).astype(BF16)
-        packed = jnp.concatenate([p.astype(F32) for p in parts3(active[8 * q : 8 * q + 8] * tension)], 0).astype(BF16)
+        packed = jnp.concatenate([p.astype(F32) for p in parts3(active[8 * q : 8 * q + 8] * tension)[:2]], 0).astype(BF16)
         total += lax.dot_general(packed, hot, NT, preferred_element_type=F32)
-    total = passive[...] + total[0:8] + total[8:16] + total[16:24]
+    total = passive[...] + total[0:8] + total[8:16]
     residual[...] = total[0:3]
 
     code = jnp.concatenate([code_col[...], code_col[...]], 1)

time: 88.6 us -> 88.7 us (level)
  no operation moved by 1% of the time
where the time goes in v4:
time: 88.7 us; the launch traced here: 88.2 us
  starting transfers between devices  40.3 us (45%)
  waiting for transfers between devices  26.3 us (30%)
  Pallas kernels  19.7 us (22%)
  local copies, waits for them, and re-layouts  0.96 us (1%)
  between operations  0.93 us (1%)
    all_to_all x2, starting transfers between devices, exchange(): lax.all_to_all(msg.reshape(256, 1, ROWS * 128), ALL, 0, 0, tiled=True)  21.9 us
    ppermute x8, starting transfers between devices, shift(): return lax.ppermute(x, axis, pairs)  18.4 us
    all_to_all x2, waiting for transfers between devices, exchange(): lax.all_to_all(msg.reshape(256, 1, ROWS * 128), ALL, 0, 0, tiled=True)  16.1 us
    pallas_call x3, Pallas kernels, call(): pl.pallas_call(body, grid=(1,), out_shape=outs, in_specs=[whole(x.shape,...  14.4 us
    ppermute x8, waiting for transfers between devices, shift(): return lax.ppermute(x, axis, pairs)  10.2 us
    pallas_call x1, Pallas kernels, shards(): pl.pallas_call(functools.partial(third_kernel, sizes), grid=(1,), out_sha...  5.29 us
  transfers between devices with their start and end apart: 10, of which 4 were waited for; matrix products, arithmetic and copies ran while one was open for 0% of the time, Pallas kernels for 2%

profile of v4, /device:TPU:1, one launch (start us, length us, event | category | flops | bytes accessed | tf_op | source)
XLA Modules:
  0.0 88.2 jit_solution(9983350171080219991)
XLA Ops:
  0.7 5.4 %first.1 = (f32[19,16,16,128]{3,2,1,0:T(8,128)}, f32[2,16,128]{2,1,0:T(8,128)}, f32[2,16,128]{2,1,0:T(8,128)}, f32[2,16,128]{2,1,0:T(8,128)}, f32[2,16,128]{2,1,...) custom-call(s32[2]{0:T(128)} %bitcast.15, s32[2]{0:T(128)} %bitcast.16, f32[17]{0:T(128)} %half_ref.3, f32[17]{0:T(128)} %slope_ref.3, ...), custom_call_target="tpu_custom_call" | custom-call | tf_op jit(solution)/shard_map/first/pallas_call | solution.py:541
  6.2 0.0 copy-start.1
  6.2 0.0 copy-start.2
  6.2 15.7 %all-to-all-start = ((f32[256,1,640]{2,1,0:T(1,128)}), f32[256,1,640]{2,1,0:T(1,128)S(1)}, u32[]{:S(2)}, u32[]{:S(2)}) async-start(f32[256,1,640]{2,1,0:T(1,128)} %bitcast.13), calls=%async_computation | async-start | bytes 1310720 | tf_op jit(solution)/shard_map/all_to_all | solution.py:527
  21.8 3.4 %collective-permute-start = (f32[2,16,128]{2,1,0:T(8,128)}, f32[2,16,128]{2,1,0:T(8,128)S(1)}, u32[]{:S(2)}, u32[]{:S(2)}) collective-permute-start(f32[2,16,128]{2,1,0:T(8,128)} %get-tuple-element.21), channel_id=1, source_target_pairs={{0,32},{32,64},{64,96},{96,128},{128,160},{160,192},{192,224},{1,3... | collective-permute-start | bytes 49160 | tf_op jit(solution)/shard_map/ppermute | solution.py:523
  25.3 1.3 %collective-permute-start.1 = (f32[2,16,128]{2,1,0:T(8,128)}, f32[2,16,128]{2,1,0:T(8,128)S(1)}, u32[]{:S(2)}, u32[]{:S(2)}) collective-permute-start(f32[2,16,128]{2,1,0:T(8,128)} %get-tuple-element.22), channel_id=1, source_target_pairs={{32,0},{64,32},{96,64},{128,96},{160,128},{192,160},{224,192},{33,... | collective-permute-start | bytes 49160 | tf_op jit(solution)/shard_map/ppermute | solution.py:523
  26.6 3.2 %collective-permute-start.2 = (f32[2,16,128]{2,1,0:T(8,128)}, f32[2,16,128]{2,1,0:T(8,128)S(1)}, u32[]{:S(2)}, u32[]{:S(2)}) collective-permute-start(f32[2,16,128]{2,1,0:T(8,128)} %get-tuple-element.23), channel_id=1, source_target_pairs={{0,8},{8,16},{16,24},{1,9},{9,17},{17,25},{2,10},{10,18},{18,26},{... | collective-permute-start | bytes 49160 | tf_op jit(solution)/shard_map/ppermute | solution.py:523
  29.7 1.3 %collective-permute-start.3 = (f32[2,16,128]{2,1,0:T(8,128)}, f32[2,16,128]{2,1,0:T(8,128)S(1)}, u32[]{:S(2)}, u32[]{:S(2)}) collective-permute-start(f32[2,16,128]{2,1,0:T(8,128)} %get-tuple-element.24), channel_id=1, source_target_pairs={{8,0},{16,8},{24,16},{9,1},{17,9},{25,17},{10,2},{18,10},{26,18},{... | collective-permute-start | bytes 49160 | tf_op jit(solution)/shard_map/ppermute | solution.py:523
  31.1 1.8 %elements.1 = (f32[64,256]{1,0:T(8,128)S(1)}, f32[8,512]{1,0:T(8,128)S(1)}, f32[64,256]{1,0:T(8,128)S(1)}) custom-call(f32[3]{0:T(128)S(1)} %copy-done.13, f32[2,64]{1,0:T(2,128)S(1)} %copy-done.6, f32[3,512]{1,0:T(4,128)S(1)} %copy-done.5, s32[8,256]{1,0:T(8,128)S(1)} %copy-done.3, s32[1,256]{1,0:T(1,128)S(1)} %bitcast.12), custom_call_target="tpu_custom_call" | custom-call | tf_op jit(solution)/shard_map/elements/pallas_call | solution.py:541
  32.8 0.0 collective-permute-done.xm
  32.9 4.2 %collective-permute-done.1.xp = f32[2,16,128]{2,1,0:T(8,128)S(1)} collective-permute-done((f32[2,16,128]{2,1,0:T(8,128)}, f32[2,16,128]{2,1,0:T(8,128)S(1)}, u32[]{:S(2)}, u32[]{:S(2)}) %collective-permute-start.1) | collective-permute-done | bytes 16416 | tf_op jit(solution)/shard_map/ppermute | solution.py:523
  37.1 0.0 collective-permute-done.2.ym
  37.1 8.1 %all-to-all-done = f32[256,1,640]{2,1,0:T(1,128)S(1)} async-done(((f32[256,1,640]{2,1,0:T(1,128)}), f32[256,1,640]{2,1,0:T(1,128)S(1)}, u32[]{:S(2)}, u32[]{:S(2)}) %all-to-all-start) | async-done | bytes 655392 | tf_op jit(solution)/shard_map/all_to_all | solution.py:527
  45.2 0.0 copy-start
  45.2 0.9 %copy-done = f32[256,128]{1,0:T(8,128)S(1)} copy-done((f32[256,128]{1,0:T(8,128)S(1)}, f32[256,128]{1,0:T(8,128)}, u32[]{:S(2)}) %copy-start) | copy-done | bytes 131096
  46.1 7.2 %second.1 = (f32[19,16,16,128]{3,2,1,0:T(8,128)}, f32[2,16,128]{2,1,0:T(8,128)S(1)}, f32[2,16,128]{2,1,0:T(8,128)S(1)}, f32[2,16,128]{2,1,0:T(8,128)S(1)}, f32[2...) custom-call(f32[17]{0:T(128)S(1)} %copy-done.7, f32[17]{0:T(128)S(1)} %copy-done.8, ...), custom_call_target="tpu_custom_call" | custom-call | tf_op jit(solution)/shard_map/second/pallas_call | solution.py:541
  53.3 6.2 %all-to-all-start.1 = ((f32[256,1,640]{2,1,0:T(1,128)}), f32[256,1,640]{2,1,0:T(1,128)S(1)}, u32[]{:S(2)}, u32[]{:S(2)}) async-start(f32[256,1,640]{2,1,0:T(1,128)} %bitcast.7), calls=%async_computation.1 | async-start | bytes 1310720 | tf_op jit(solution)/shard_map/all_to_all | solution.py:527
  59.5 3.5 %collective-permute-start.4 = (f32[2,16,128]{2,1,0:T(8,128)S(1)}, f32[2,16,128]{2,1,0:T(8,128)S(1)}, u32[]{:S(2)}, u32[]{:S(2)}) collective-permute-start(f32[2,16,128]{2,1,0:T(8,128)S(1)} %get-tuple-element.29), channel_id=1, source_target_pairs={{0,32},{32,64},{64,96},{96,128},{128,160},{160,192},{192,224},{1,3... | collective-permute-start | bytes 49160 | tf_op jit(solution)/shard_map/ppermute | solution.py:523
  63.0 1.3 %collective-permute-start.5 = (f32[2,16,128]{2,1,0:T(8,128)S(1)}, f32[2,16,128]{2,1,0:T(8,128)S(1)}, u32[]{:S(2)}, u32[]{:S(2)}) collective-permute-start(f32[2,16,128]{2,1,0:T(8,128)S(1)} %get-tuple-element.30), channel_id=1, source_target_pairs={{32,0},{64,32},{96,64},{128,96},{160,128},{192,160},{224,192},{33,... | collective-permute-start | bytes 49160 | tf_op jit(solution)/shard_map/ppermute | solution.py:523
  64.3 3.2 %collective-permute-start.6 = (f32[2,16,128]{2,1,0:T(8,128)S(1)}, f32[2,16,128]{2,1,0:T(8,128)S(1)}, u32[]{:S(2)}, u32[]{:S(2)}) collective-permute-start(f32[2,16,128]{2,1,0:T(8,128)S(1)} %get-tuple-element.31), channel_id=1, source_target_pairs={{0,8},{8,16},{16,24},{1,9},{9,17},{17,25},{2,10},{10,18},{18,26},{... | collective-permute-start | bytes 49160 | tf_op jit(solution)/shard_map/ppermute | solution.py:523
  67.5 1.3 %collective-permute-start.7 = (f32[2,16,128]{2,1,0:T(8,128)S(1)}, f32[2,16,128]{2,1,0:T(8,128)S(1)}, u32[]{:S(2)}, u32[]{:S(2)}) collective-permute-start(f32[2,16,128]{2,1,0:T(8,128)S(1)} %get-tuple-element.32), channel_id=1, source_target_pairs={{8,0},{16,8},{24,16},{9,1},{17,9},{25,17},{10,2},{18,10},{26,18},{... | collective-permute-start | bytes 49160 | tf_op jit(solution)/shard_map/ppermute | solution.py:523
  68.8 6.0 %collective-permute-done.5.xp = f32[2,16,128]{2,1,0:T(8,128)S(1)} collective-permute-done((f32[2,16,128]{2,1,0:T(8,128)S(1)}, f32[2,16,128]{2,1,0:T(8,128)S(1)}, u32[]{:S(2)}, u32[]{:S(2)}) %collective-permute-start.5) | collective-permute-done | bytes 16416 | tf_op jit(solution)/shard_map/ppermute | solution.py:523
  74.8 8.1 %all-to-all-done.1 = f32[256,1,640]{2,1,0:T(1,128)S(1)} async-done(((f32[256,1,640]{2,1,0:T(1,128)}), f32[256,1,640]{2,1,0:T(1,128)S(1)}, u32[]{:S(2)}, u32[]{:S(2)}) %all-to-all-start.1) | async-done | bytes 655392 | tf_op jit(solution)/shard_map/all_to_all | solution.py:527
  82.9 5.3 %third.1 = (f32[19,16,16,128]{3,2,1,0:T(8,128)}, f32[3,16,16,128]{3,2,1,0:T(8,128)}, f32[3,512]{1,0:T(4,128)}) custom-call(f32[19,16,16,128]{3,2,1,0:T(8,128)} %get-tuple-element.28.s2, f32[2,16,128]{2,1,0:T(8,128)S(1)} %collective-permute-done.4.xm, f32[2,16,128]{2,1,0:T(8,128)S(1)} %collective-permute-done.5.xp, ...), custom_call_target="tpu_custom_call", output_to_operand_aliasing={{0}: (0, {})} | custom-call | tf_op jit(solution)/shard_map/third/pallas_call | solution.py:615
  (28 shorter events, 0.1 us)
Async XLA Ops:
  0.6 44.5 %copy-start.11 = (f32[17]{0:T(128)S(1)}, f32[17]{0:T(128)}, u32[]{:S(2)}) copy-start(f32[17]{0:T(128)} %rev_ref.3) | copy-start | bytes 208
  0.6 44.5 %copy-start.10 = (f32[17]{0:T(128)S(1)}, f32[17]{0:T(128)}, u32[]{:S(2)}) copy-start(f32[17]{0:T(128)} %cond_ref.3) | copy-start | bytes 208
  0.7 44.5 %copy-start.9 = (f32[17]{0:T(128)S(1)}, f32[17]{0:T(128)}, u32[]{:S(2)}) copy-start(f32[17]{0:T(128)} %tau_ref.3) | copy-start | bytes 208
  0.7 44.5 %copy-start.8 = (f32[17]{0:T(128)S(1)}, f32[17]{0:T(128)}, u32[]{:S(2)}) copy-start(f32[17]{0:T(128)} %slope_ref.3) | copy-start | bytes 208
  0.7 44.5 %copy-start.7 = (f32[17]{0:T(128)S(1)}, f32[17]{0:T(128)}, u32[]{:S(2)}) copy-start(f32[17]{0:T(128)} %half_ref.3) | copy-start | bytes 208
  0.7 30.3 %copy-start.6 = (f32[2,64]{1,0:T(2,128)S(1)}, f32[2,64]{1,0:T(2,128)}, u32[]{:S(2)}) copy-start(f32[2,64]{1,0:T(2,128)} %angle.3) | copy-start | bytes 1540
  0.7 30.3 %copy-start.3 = (s32[8,256]{1,0:T(8,128)S(1)}, s32[8,256]{1,0:T(8,128)}, u32[]{:S(2)}) copy-start(s32[8,256]{1,0:T(8,128)} %elem_node.3) | copy-start | bytes 24580
  0.7 30.3 %copy-start.13 = (f32[3]{0:T(128)S(1)}, f32[3]{0:T(128)}, u32[]{:S(2)}) copy-start(f32[3]{0:T(128)} %material.1) | copy-start | bytes 40
  0.7 30.3 %copy-start.12 = (s32[256]{0:T(256)S(1)}, s32[256]{0:T(256)}, u32[]{:S(2)}) copy-start(s32[256]{0:T(256)} %param.31) | copy-start | bytes 3076
  0.7 30.3 %copy-start.5 = (f32[3,512]{1,0:T(4,128)S(1)}, f32[3,512]{1,0:T(4,128)}, u32[]{:S(2)}) copy-start(f32[3,512]{1,0:T(4,128)} %node_disp.1) | copy-start | bytes 18436
  0.7 44.4 %copy-start.4 = (f32[8,8,4]{1,2,0:T(4,128)S(1)}, f32[8,8,4]{1,2,0:T(4,128)}, u32[]{:S(2)}) copy-start(f32[8,8,4]{1,2,0:T(4,128)} %param.28) | copy-start | bytes 3076
  6.2 76.7 %copy-start.1 = (f32[256,128]{1,0:T(8,128)S(1)}, f32[256,128]{1,0:T(8,128)}, u32[]{:S(2)}) copy-start(f32[256,128]{1,0:T(8,128)} %get-tuple-element.27.code_col) | copy-start | bytes 393220
  6.2 76.7 %copy-start.2 = (bf16[2,256,512]{2,1,0:T(8,128)(2,1)S(1)}, bf16[2,256,512]{2,1,0:T(8,128)(2,1)}, u32[]{:S(2)}) copy-start(bf16[2,256,512]{2,1,0:T(8,128)(2,1)} %constant.2.clone.blend_hbm) | copy-start | bytes 1572868
  6.2 38.9 %all-to-all-start = ((f32[256,1,640]{2,1,0:T(1,128)}), f32[256,1,640]{2,1,0:T(1,128)S(1)}, u32[]{:S(2)}, u32[]{:S(2)}) async-start(f32[256,1,640]{2,1,0:T(1,128)} %bitcast.13), calls=%async_computation | async-start | bytes 1310720 | tf_op jit(solution)/shard_map/all_to_all | solution.py:527
  21.8 11.0 %collective-permute-start = (f32[2,16,128]{2,1,0:T(8,128)}, f32[2,16,128]{2,1,0:T(8,128)S(1)}, u32[]{:S(2)}, u32[]{:S(2)}) collective-permute-start(f32[2,16,128]{2,1,0:T(8,128)} %get-tuple-element.21), channel_id=1, source_target_pairs={{0,32},{32,64},{64,96},{96,128},{128,160},{160,192},{192,224},{1,3... | collective-permute-start | bytes 49160 | tf_op jit(solution)/shard_map/ppermute | solution.py:523
  25.3 11.8 %collective-permute-start.1 = (f32[2,16,128]{2,1,0:T(8,128)}, f32[2,16,128]{2,1,0:T(8,128)S(1)}, u32[]{:S(2)}, u32[]{:S(2)}) collective-permute-start(f32[2,16,128]{2,1,0:T(8,128)} %get-tuple-element.22), channel_id=1, source_target_pairs={{32,0},{64,32},{96,64},{128,96},{160,128},{192,160},{224,192},{33,... | collective-permute-start | bytes 49160 | tf_op jit(solution)/shard_map/ppermute | solution.py:523
  26.6 10.5 %collective-permute-start.2 = (f32[2,16,128]{2,1,0:T(8,128)}, f32[2,16,128]{2,1,0:T(8,128)S(1)}, u32[]{:S(2)}, u32[]{:S(2)}) collective-permute-start(f32[2,16,128]{2,1,0:T(8,128)} %get-tuple-element.23), channel_id=1, source_target_pairs={{0,8},{8,16},{16,24},{1,9},{9,17},{17,25},{2,10},{10,18},{18,26},{... | collective-permute-start | bytes 49160 | tf_op jit(solution)/shard_map/ppermute | solution.py:523
  29.7 7.3 %collective-permute-start.3 = (f32[2,16,128]{2,1,0:T(8,128)}, f32[2,16,128]{2,1,0:T(8,128)S(1)}, u32[]{:S(2)}, u32[]{:S(2)}) collective-permute-start(f32[2,16,128]{2,1,0:T(8,128)} %get-tuple-element.24), channel_id=1, source_target_pairs={{8,0},{16,8},{24,16},{9,1},{17,9},{25,17},{10,2},{18,10},{26,18},{... | collective-permute-start | bytes 49160 | tf_op jit(solution)/shard_map/ppermute | solution.py:523
  45.2 0.9 %copy-start = (f32[256,128]{1,0:T(8,128)S(1)}, f32[256,128]{1,0:T(8,128)}, u32[]{:S(2)}) copy-start(f32[256,128]{1,0:T(8,128)} %get-tuple-element.27.code_col) | copy-start | bytes 393220
  53.3 29.6 %all-to-all-start.1 = ((f32[256,1,640]{2,1,0:T(1,128)}), f32[256,1,640]{2,1,0:T(1,128)S(1)}, u32[]{:S(2)}, u32[]{:S(2)}) async-start(f32[256,1,640]{2,1,0:T(1,128)} %bitcast.7), calls=%async_computation.1 | async-start | bytes 1310720 | tf_op jit(solution)/shard_map/all_to_all | solution.py:527
  59.5 9.3 %collective-permute-start.4 = (f32[2,16,128]{2,1,0:T(8,128)S(1)}, f32[2,16,128]{2,1,0:T(8,128)S(1)}, u32[]{:S(2)}, u32[]{:S(2)}) collective-permute-start(f32[2,16,128]{2,1,0:T(8,128)S(1)} %get-tuple-element.29), channel_id=1, source_target_pairs={{0,32},{32,64},{64,96},{96,128},{128,160},{160,192},{192,224},{1,3... | collective-permute-start | bytes 49160 | tf_op jit(solution)/shard_map/ppermute | solution.py:523
  63.0 11.8 %collective-permute-start.5 = (f32[2,16,128]{2,1,0:T(8,128)S(1)}, f32[2,16,128]{2,1,0:T(8,128)S(1)}, u32[]{:S(2)}, u32[]{:S(2)}) collective-permute-start(f32[2,16,128]{2,1,0:T(8,128)S(1)} %get-tuple-element.30), channel_id=1, source_target_pairs={{32,0},{64,32},{96,64},{128,96},{160,128},{192,160},{224,192},{33,... | collective-permute-start | bytes 49160 | tf_op jit(solution)/shard_map/ppermute | solution.py:523
  64.3 10.5 %collective-permute-start.6 = (f32[2,16,128]{2,1,0:T(8,128)S(1)}, f32[2,16,128]{2,1,0:T(8,128)S(1)}, u32[]{:S(2)}, u32[]{:S(2)}) collective-permute-start(f32[2,16,128]{2,1,0:T(8,128)S(1)} %get-tuple-element.31), channel_id=1, source_target_pairs={{0,8},{8,16},{16,24},{1,9},{9,17},{17,25},{2,10},{10,18},{18,26},{... | collective-permute-start | bytes 49160 | tf_op jit(solution)/shard_map/ppermute | solution.py:523
  67.5 7.3 %collective-permute-start.7 = (f32[2,16,128]{2,1,0:T(8,128)S(1)}, f32[2,16,128]{2,1,0:T(8,128)S(1)}, u32[]{:S(2)}, u32[]{:S(2)}) collective-permute-start(f32[2,16,128]{2,1,0:T(8,128)S(1)} %get-tuple-element.32), channel_id=1, source_target_pairs={{8,0},{16,8},{24,16},{9,1},{17,9},{25,17},{10,2},{18,10},{26,18},{... | collective-permute-start | bytes 49160 | tf_op jit(solution)/shard_map/ppermute | solution.py:523
